TPU v7x, 128 devices: a whole 4x4x4 slice. The times are simulated.
128 devices in a mesh: str: 16 (over x_lo, y, core), crs: 8 (over x_hi, z).
Axes of the slice: x: 4 (x_hi: 2, x_lo: 2; x = x_hi * 2 + x_lo), y: 4, z: 4, core: 2. Of those that a mesh axis runs over, the one named last changes fastest.
Arguments:
- voltage: float32 [4, 512, 16384], P(None, 'str', 'crs'), may hold values from -4 to 0.5
- photocurrent: float32 [4, 512, 16384], P(None, 'str', 'crs'), may hold values from 0.1 to 10
- shunt: float32 [512, 16384], P('str', 'crs'), may hold values from 0.02 to 0.5
- series: float32 [512, 16384], P('str', 'crs'), may hold values from 0.5 to 2
- pattern: int32 [512, 128], P('str', 'crs'), may hold values from 0 to 3
- diode_mask: int32 [512, 128], P('str', 'crs'), may hold values 0 or 1
- aggregate: int32 [512, 128], P('str', 'crs'), may hold values from 0 to 4095, as said below
- coarse_inverse: float32 [4096, 4096], P('crs'), as said below
Outputs:
- newton_step: float32 [4, 512, 16384], P(None, 'str', 'crs')
- residual: float32 [4, 512, 16384], P(None, 'str', 'crs')
Inputs may be any that keep to these rules, and one draw needn't show every extreme that they name: `aggregate`: every value appears. coarse_inverse is symmetric positive definite.
All inputs are finite; a program needn't handle non-finite values. No bound on the sum of `diode_mask` on one device may be relied on, other than what follows from the above.
Results may differ from a plain program's by a relative error of at most 0.0003.
Values sent between devices are 32-bit elements; how exact they have to be, the bound alone decides.
A program may use at most 64 MiB of HBM per device.

v0:
```python
import jax
import jax.numpy as jnp
from jax import lax
from jax.sharding import PartitionSpec as P

ITERS = 3


LEVELS = (0.25, 0.5, 1.0, 2.0)
DIODE_SAT = 0.5


def with_halo(block, sides, width, periodic):
    for axis, dim in sides:
        count = lax.axis_size(axis)
        forward = [(i, i + 1) for i in range(count - 1)]
        if periodic:
            forward.append((count - 1, 0))
        backward = [(target, source) for source, target in forward]
        low = lax.ppermute(
            lax.slice_in_dim(block, block.shape[dim] - width, None, axis=dim), axis, forward
        )
        high = lax.ppermute(lax.slice_in_dim(block, 0, width, axis=dim), axis, backward)
        block = jnp.concatenate([low, block, high], axis=dim)
    return block


def widen(blocks):
    shape = blocks.shape
    spread = jnp.broadcast_to(blocks[..., None], shape + (128,))
    return spread.reshape(shape[:-1] + (shape[-1] * 128,))


def cross_levels(pattern):
    total = jnp.zeros(pattern.shape, jnp.float32)
    for number in range(4):
        total = total + jnp.where(pattern == number, jnp.float32(LEVELS[number]), jnp.float32(0.0))
    return total


def neighbours(field):
    along = with_halo(field, (("str", 1),), 1, True)
    across = with_halo(field, (("crs", 2),), 1, False)
    return (along[:, 2:], along[:, :-2], across[:, :, 2:], across[:, :, :-2])


def shards(voltage, photocurrent, shunt, series, pattern, diode_mask, aggregate, coarse_inverse):
    points = voltage.shape[0]
    rows_here = voltage.shape[1]
    local_block_list = voltage.shape[2] // 128
    coarse_count = coarse_inverse.shape[1]
    cross_level = widen(cross_levels(pattern))
    diode_area = widen(diode_mask.astype(jnp.float32))
    flat_groups = aggregate.reshape(-1)
    stacked = jnp.concatenate([voltage, cross_level[None], series[None]], axis=0)
    below, above, right_cells, left_cells = neighbours(stacked)
    right_link = jnp.minimum(cross_level, right_cells[points])
    left_link = jnp.minimum(cross_level, left_cells[points])
    up_link = above[points + 1]
    diode_derivative = DIODE_SAT * diode_area * jnp.exp(voltage)
    imbalance = (
        shunt * voltage
        + series * (voltage - below[:points])
        + up_link * (voltage - above[:points])
        + right_link * (voltage - right_cells[:points])
        + left_link * (voltage - left_cells[:points])
        + diode_derivative
        - DIODE_SAT * diode_area
        - photocurrent
    )
    diagonal = shunt + diode_derivative + series + up_link + right_link + left_link

    def restrict(remainder):
        block_sums = remainder.reshape(points, rows_here * local_block_list, 128).sum(axis=-1)
        return jax.ops.segment_sum(block_sums.T, flat_groups, num_segments=coarse_count).T

    def interpolate_upward(correction):
        picked = jnp.take(correction, flat_groups, axis=1)
        return widen(picked.reshape(points, rows_here, local_block_list))

    def coarse_solve(incomplete_value):
        product = None
        total = lax.psum(incomplete_value, ("str", "crs"))
        row_share = lax.dot_general(
            total, coarse_inverse, (((1,), (1,)), ((), ())), precision=lax.Precision.HIGHEST
        )
        correction = lax.all_gather(row_share, "crs", axis=1, tiled=True)
        return (correction, product)

    def precondition(remainder):
        resident_portion = remainder / diagonal
        incomplete_value = restrict(remainder)
        correction, product = coarse_solve(incomplete_value)
        smoothed = resident_portion + interpolate_upward(correction)
        product = lax.psum(jnp.sum(remainder * smoothed, axis=(1, 2)), ("str", "crs"))
        return (smoothed, product)

    remainder = -imbalance
    newton_step = jnp.zeros_like(voltage)
    smoothed, product = precondition(remainder)
    direction = smoothed
    for turn in range(ITERS):
        operate_below, operate_above, operate_right_cells, operate_left_cells = neighbours(
            direction
        )
        image = (
            diagonal * direction
            - series * operate_below
            - up_link * operate_above
            - right_link * operate_right_cells
            - left_link * operate_left_cells
        )
        curvature = lax.psum(jnp.sum(direction * image, axis=(1, 2)), ("str", "crs"))
        alpha = (product / curvature)[:, None, None]
        newton_step = newton_step + alpha * direction
        remainder = remainder - alpha * image
        if turn + 1 < ITERS:
            smoothed, fresh = precondition(remainder)
            ratio = (fresh / product)[:, None, None]
            direction = smoothed + ratio * direction
            product = fresh
    return (newton_step, remainder)


def solution(mesh):
    placed = (
        P(None, "str", "crs"),
        P(None, "str", "crs"),
        P("str", "crs"),
        P("str", "crs"),
        P("str", "crs"),
        P("str", "crs"),
        P("str", "crs"),
        P("crs", None),
    )
    return jax.shard_map(
        shards,
        mesh=mesh,
        in_specs=placed,
        out_specs=(P(None, "str", "crs"), P(None, "str", "crs")),
        check_vma=False,
    )
```

profile of v0, /device:TPU:1, one launch (start us, length us, event | category | flops | bytes accessed | tf_op | source)
XLA Modules:
  0.0 1062.7 jit_solution(3380685636923150555)
XLA Ops:
  9.5 1.5 collective-permute-start
  11.0 1.3 collective-permute-start.1
  13.7 4.2 collective-permute-start.3
  20.6 2.9 fusion.30
  24.8 1.6 reduce_sum.81
  26.5 3.8 scatter_custom_fusion
  30.4 158.7 %all-reduce.5.cloned.1.call-done = f32[4,4096]{0,1:T(8,128)} async-done(((f32[4,4096]{0,1:T(8,128)}), f32[4,4096]{0,1:T(8,128)}) %all-reduce.5.cloned.1.call-update) | async-done | bytes 65552 | tf_op jit(solution)/shard_map/psum | solution.py:83
  189.0 10.9 %fusion.54 = f32[4,512]{1,0:T(4,128)S(1)} fusion(f32[4,4096]{0,1:T(8,128)} %all-reduce.5.cloned.1.call-done, f32[512,4096]{1,0:T(8,128)} %param.17), kind=kOutput, calls=%fused_computation.118 | convolution fusion | flops 100663296 | bytes 8462336 | tf_op jit(solution)/shard_map/dot_general | solution.py:84
  199.9 28.2 %all_gather.9 = f32[4,4096]{1,0:T(4,128)S(1)} all-gather(f32[4,512]{1,0:T(4,128)S(1)} %fusion.54), channel_id=1, replica_groups=mesh['str'=16,'crs'=8] {'crs'}, dimensions={1}, use_global_device_ids=true | all-gather | bytes 73728 | tf_op jit(solution)/shard_map/all_gather | solution.py:87
  228.8 1.6 gather_fusion
  233.3 2.6 divide_add_fusion.2
  235.9 7.2 collective-permute-start.4
  245.7 4.0 collective-permute-start.7
  249.8 1.8 collective-permute-done.7
  252.6 69.2 %all-reduce = (f32[4]{0:T(128)}, f32[4]{0:T(128)}) all-reduce(f32[4]{0:T(128)S(1)} %get-tuple-element.4, f32[4]{0:T(128)S(1)} %get-tuple-element.3), channel_id=1, replica_groups=mesh['str'=16,'crs'=8] {'str','crs'}, use_global_device_ids=true, to_apply=%region_4.6 | all-reduce | flops 8 | bytes 64 | tf_op jit(solution)/shard_map/psum | solution.py:95
  322.5 2.8 multiply_subtract_fusion.2
  325.3 1.4 reshape.56
  327.2 3.8 scatter_custom_fusion.1
  331.6 147.1 %all-reduce.7.cloned.1.call-done = f32[4,4096]{0,1:T(8,128)} async-done(((f32[4,4096]{0,1:T(8,128)}), f32[4,4096]{0,1:T(8,128)}) %all-reduce.7.cloned.1.call-update) | async-done | bytes 65552 | tf_op jit(solution)/shard_map/psum | solution.py:83
  478.7 10.9 %fusion.55 = f32[4,512]{1,0:T(4,128)S(1)} fusion(f32[4,4096]{0,1:T(8,128)} %all-reduce.7.cloned.1.call-done, f32[512,4096]{1,0:T(8,128)} %param.17), kind=kOutput, calls=%fused_computation.119 | convolution fusion | flops 100663296 | bytes 8462336 | tf_op jit(solution)/shard_map/dot_general | solution.py:84
  489.6 27.8 %all_gather.10 = f32[4,4096]{1,0:T(4,128)S(1)} all-gather(f32[4,512]{1,0:T(4,128)S(1)} %fusion.55), channel_id=1, replica_groups=mesh['str'=16,'crs'=8] {'crs'}, dimensions={1}, use_global_device_ids=true | all-gather | bytes 73728 | tf_op jit(solution)/shard_map/all_gather | solution.py:87
  517.4 2.0 copy.34
  519.4 3.3 gather_fusion.1
  522.7 1.8 broadcast_select_fusion.1
  527.0 2.4 reshape.57
  529.4 1.6 multiply_reduce_fusion.3
  531.0 70.0 %psum.67 = f32[4]{0:T(128)S(1)} all-reduce(f32[4]{0:T(128)S(1)} %multiply_reduce_fusion.3), channel_id=1, replica_groups=mesh['str'=16,'crs'=8] {'str','crs'}, use_global_device_ids=true, to_apply=%region_11.13 | all-reduce | flops 4 | bytes 32 | tf_op jit(solution)/shard_map/psum | solution.py:95
  601.0 1.9 multiply_add_fusion.2
  606.1 4.0 collective-permute-start.11
  613.5 71.2 %psum.68 = f32[4]{0:T(128)} all-reduce(f32[4]{0:T(128)S(1)} %multiply_reduce_fusion.2), channel_id=1, replica_groups=mesh['str'=16,'crs'=8] {'str','crs'}, use_global_device_ids=true, to_apply=%region_13.15 | all-reduce | flops 4 | bytes 32 | tf_op jit(solution)/shard_map/psum | solution.py:113
  685.2 3.1 multiply_subtract_fusion.1
  688.4 2.4 reshape.58
  690.7 1.6 reduce_sum.87
  693.1 4.1 scatter_custom_fusion.2
  697.2 147.4 %all-reduce.9.cloned.1.call-done = f32[4,4096]{0,1:T(8,128)} async-done(((f32[4,4096]{0,1:T(8,128)}), f32[4,4096]{0,1:T(8,128)}) %all-reduce.9.cloned.1.call-update) | async-done | bytes 65552 | tf_op jit(solution)/shard_map/psum | solution.py:83
  844.6 10.9 %fusion.56 = f32[4,512]{1,0:T(4,128)S(1)} fusion(f32[4,4096]{0,1:T(8,128)} %all-reduce.9.cloned.1.call-done, f32[512,4096]{1,0:T(8,128)} %param.17), kind=kOutput, calls=%fused_computation.120 | convolution fusion | flops 100663296 | bytes 8462336 | tf_op jit(solution)/shard_map/dot_general | solution.py:84
  855.5 27.8 %all_gather.11 = f32[4,4096]{1,0:T(4,128)S(1)} all-gather(f32[4,512]{1,0:T(4,128)S(1)} %fusion.56), channel_id=1, replica_groups=mesh['str'=16,'crs'=8] {'crs'}, dimensions={1}, use_global_device_ids=true | all-gather | bytes 73728 | tf_op jit(solution)/shard_map/all_gather | solution.py:87
  883.3 2.0 copy.37
  885.3 3.2 gather_fusion.2
  888.5 1.8 broadcast_select_fusion
  892.9 2.4 reshape.59
  895.3 1.9 multiply_reduce_fusion.1
  897.1 70.2 %psum.70 = f32[4]{0:T(128)S(1)} all-reduce(f32[4]{0:T(128)S(1)} %multiply_reduce_fusion.1), channel_id=1, replica_groups=mesh['str'=16,'crs'=8] {'str','crs'}, use_global_device_ids=true, to_apply=%region_18.20 | all-reduce | flops 4 | bytes 32 | tf_op jit(solution)/shard_map/psum | solution.py:95
  967.3 1.9 multiply_add_fusion.1
  972.5 4.0 collective-permute-start.15
  979.8 71.0 %psum.71 = f32[4]{0:T(128)} all-reduce(f32[4]{0:T(128)S(1)} %multiply_reduce_fusion), channel_id=1, replica_groups=mesh['str'=16,'crs'=8] {'str','crs'}, use_global_device_ids=true, to_apply=%region_20.22 | all-reduce | flops 4 | bytes 32 | tf_op jit(solution)/shard_map/psum | solution.py:113
  1051.5 2.7 multiply_add_fusion
  1054.2 1.7 multiply_subtract_fusion
  (160 shorter events, 37.1 us)
Async XLA Ops:
  7.2 5.2 copy-start.1
  7.2 5.1 copy-start
  7.2 181.9 %all-reduce.5.cloned.1.call-start = ((), (), s32[]{:S(2)}) async-start(), calls=%async_computation | async-start | bytes 4194304 | tf_op jit(solution)/shard_map/psum | solution.py:83
  8.1 9.8 copy-start.39
  8.1 9.8 copy-start.37
  9.5 10.3 collective-permute-start
  11.0 8.6 collective-permute-start.1
  12.4 7.1 collective-permute-start.2
  13.7 5.8 collective-permute-start.3
  19.8 3.7 copy-start.7
  19.8 3.7 copy-start.12
  19.8 3.7 copy-start.17
  23.5 6.8 copy-start.3
  26.5 3.9 copy-start.38
  30.3 448.4 %all-reduce.7.cloned.1.call-start = ((), (), s32[]{:S(2)}) async-start(), calls=%async_computation.1 | async-start | bytes 4194304 | tf_op jit(solution)/shard_map/psum | solution.py:83
  199.9 30.5 %copy-start.36 = (pred[512]{0:T(512)(128)(4,1)S(1)}, pred[512]{0:T(512)(128)(4,1)}, u32[]{:S(2)}) copy-start(pred[512]{0:T(512)(128)(4,1)} %compare_and_fusion) | copy-start | bytes 1540
  233.3 18.4 %copy-start.4 = (f32[4,32,2048]{2,1,0:T(8,128)S(1)}, f32[4,32,2048]{2,1,0:T(8,128)}, u32[]{:S(2)}) copy-start(f32[4,32,2048]{2,1,0:T(8,128)} %copy-done.3) | copy-start | bytes 3145732
  233.3 18.4 %copy-start.8 = (f32[32,2048]{1,0:T(8,128)S(1)}, f32[32,2048]{1,0:T(8,128)}, u32[]{:S(2)}) copy-start(f32[32,2048]{1,0:T(8,128)} %copy-done.7) | copy-start | bytes 786436
  233.3 18.4 %copy-start.13 = (f32[32,2048]{1,0:T(8,128)S(1)}, f32[32,2048]{1,0:T(8,128)}, u32[]{:S(2)}) copy-start(f32[32,2048]{1,0:T(8,128)} %copy-done.12) | copy-start | bytes 786436
  233.3 18.4 %copy-start.18 = (f32[32,2048]{1,0:T(8,128)S(1)}, f32[32,2048]{1,0:T(8,128)}, u32[]{:S(2)}) copy-start(f32[32,2048]{1,0:T(8,128)} %copy-done.17) | copy-start | bytes 786436
  235.9 15.7 %collective-permute-start.4 = (f32[4,1,2048]{2,1,0:T(1,128)S(1)}, f32[4,1,2048]{2,1,0:T(1,128)S(1)}, u32[]{:S(2)}, u32[]{:S(2)}) collective-permute-start(f32[4,1,2048]{2,1,0:T(1,128)S(1)} %get-tuple-element.24), channel_id=1, source_target_pairs={{8,0},{16,8},{24,16},{32,24},{40,32},{48,40},{56,48},{64,56},{72,6... | collective-permute-start | bytes 98312 | tf_op jit(solution)/shard_map/ppermute | solution.py:23
  243.1 8.6 collective-permute-start.5
  244.5 5.4 collective-permute-start.6
  245.7 5.9 collective-permute-start.7
  251.7 70.8 %copy-start.5 = (f32[4,32,2048]{2,1,0:T(8,128)S(1)}, f32[4,32,2048]{2,1,0:T(8,128)}, u32[]{:S(2)}) copy-start(f32[4,32,2048]{2,1,0:T(8,128)} %copy-done.3) | copy-start | bytes 3145732
  331.0 513.7 %all-reduce.9.cloned.1.call-start = ((), (), s32[]{:S(2)}) async-start(), calls=%async_computation.2 | async-start | bytes 4194304 | tf_op jit(solution)/shard_map/psum | solution.py:83
  519.4 10.0 copy-start.6
  529.4 71.5 %copy-start.42 = (f32[4]{0:T(128)S(1)}, f32[4]{0:T(128)}, u32[]{:S(2)}) copy-start(f32[4]{0:T(128)} %get-tuple-element.5) | copy-start | bytes 52
  600.9 11.7 %copy-start.9 = (f32[32,2048]{1,0:T(8,128)S(1)}, f32[32,2048]{1,0:T(8,128)}, u32[]{:S(2)}) copy-start(f32[32,2048]{1,0:T(8,128)} %copy-done.7) | copy-start | bytes 786436
  600.9 11.7 %copy-start.14 = (f32[32,2048]{1,0:T(8,128)S(1)}, f32[32,2048]{1,0:T(8,128)}, u32[]{:S(2)}) copy-start(f32[32,2048]{1,0:T(8,128)} %copy-done.12) | copy-start | bytes 786436
  600.9 11.7 %copy-start.19 = (f32[32,2048]{1,0:T(8,128)S(1)}, f32[32,2048]{1,0:T(8,128)}, u32[]{:S(2)}) copy-start(f32[32,2048]{1,0:T(8,128)} %copy-done.17) | copy-start | bytes 786436
  602.9 8.5 collective-permute-start.8
  604.1 7.3 collective-permute-start.9
  604.8 5.7 collective-permute-start.10
  606.1 5.3 collective-permute-start.11
  895.3 72.0 %copy-start.41 = (f32[4]{0:T(128)S(1)}, f32[4]{0:T(128)}, u32[]{:S(2)}) copy-start(f32[4]{0:T(128)} %copy-done.40) | copy-start | bytes 52
  967.3 11.7 %copy-start.10 = (f32[32,2048]{1,0:T(8,128)S(1)}, f32[32,2048]{1,0:T(8,128)}, u32[]{:S(2)}) copy-start(f32[32,2048]{1,0:T(8,128)} %copy-done.7) | copy-start | bytes 786436
  967.3 11.7 %copy-start.15 = (f32[32,2048]{1,0:T(8,128)S(1)}, f32[32,2048]{1,0:T(8,128)}, u32[]{:S(2)}) copy-start(f32[32,2048]{1,0:T(8,128)} %copy-done.12) | copy-start | bytes 786436
  967.3 11.7 %copy-start.20 = (f32[32,2048]{1,0:T(8,128)S(1)}, f32[32,2048]{1,0:T(8,128)}, u32[]{:S(2)}) copy-start(f32[32,2048]{1,0:T(8,128)} %copy-done.17) | copy-start | bytes 786436
  969.2 8.6 copy-start.22
  969.3 8.5 collective-permute-start.12
  970.5 7.3 collective-permute-start.13
  971.2 5.7 collective-permute-start.14
  972.5 5.3 collective-permute-start.15
  1051.5 2.7 copy-start.21
  1051.5 2.7 copy-start.23
  1051.5 2.7 copy-start.27
  1051.5 2.7 copy-start.30
  (14 other events, 17.6 us)
Sparse Core Ops, SparseCore 0:
  30.4 158.5 all-reduce.4
  331.1 147.5 all-reduce.6
  697.4 147.2 all-reduce.8
where the time goes:
time: 1070 us; the launch traced here: 1060 us
  waiting for transfers between devices  458 us (43%)
  blocking collectives  435 us (41%)
  other arithmetic  50.6 us (5%)
  starting transfers between devices  36.8 us (3%)
  local copies, waits for them, and re-layouts  35 us (3%)
  matrix products  32.6 us (3%)
  between operations  14.6 us (1%)
    psum x3, waiting for transfers between devices, coarse_solve(): total = lax.psum(incomplete_value, ('str', 'crs'))  453 us
    psum x3, blocking collectives, precondition(): lax.psum(jnp.sum(remainder * smoothed, axis=(1, 2)), ('str', 'crs'))  209 us
    psum x2, blocking collectives, shards(): lax.psum(jnp.sum(direction * image, axis=(1, 2)), ('str', 'crs'))  142 us
    all_gather x3, blocking collectives, coarse_solve(): correction = lax.all_gather(row_share, 'crs', axis=1, tiled=True)  83.9 us
    dot_general x3, matrix products, coarse_solve(): lax.dot_general(total, coarse_inverse, (((1,), (1,)), ((), ())), precisio...  32.6 us
  transfers between devices with their start and end apart: 19, of which 9 were waited for; matrix products, arithmetic and copies ran while one was open for 0% of the time, Pallas kernels for 0%

commit v1 on v0

v1 whole, which is shorter than its diff:
```python
import jax
import jax.numpy as jnp
from jax import lax
from jax.experimental import pallas as pl
from jax.experimental.pallas import tpu as pltpu
from jax.sharding import PartitionSpec as P

MESH = pl.DeviceIdType.MESH
F32 = jnp.float32
BF16 = jnp.bfloat16

CASES = 4
ROWS = 32
BLOCKS = 16
STEP = 40
FIELD = (BLOCKS + 2) * STEP
NS = 16
NC = 8
SOLVES = 3
LEVELS = (0.25, 0.5, 1.0, 2.0)


def dot(a, b):
    return jnp.dot(a, b, preferred_element_type=F32)


def halves(x):
    high = x.astype(BF16)
    return high, (x - high.astype(F32)).astype(BF16)


def kernel(
    v_in, photo_in, shunt_in, series_in, pattern_in, mask_in, group_in, inverse_in,
    step_out, rest_out,
    vn, pn, shn, sn, patn, maskn, groupn, staged, a_high, a_low,
    ef, rf, qf, df, xf, uf, wf, dgf, inf, pcf,
    sf, rlf, llf, dmf,
    cb, gm, e_low, m_high, groups, e_turn, ones_pair, ones_wide,
    bu, bw, bq, sd, ss, su, er, el, lb,
    pk, su_s, sd_s, sl_s, sr_s, su_r, sd_r, sl_r, sr_r,
    hu_s, hd_s, hl_s, hr_s, hu_r, hd_r, hl_r, hr_r,
    s1, r1, s2, r2, s3, r3, s4, r4, f1s, f1r, f2s, f2r,
    y_now, t_now, t_tile, state, per_case,
    in_sem, out_sem, setup_send, setup_recv, halo_send, halo_recv, send_sem, recv_sem, last_send, last_recv,
):
    s = lax.axis_index("str")
    c = lax.axis_index("crs")

    def at_str(k):
        return (lax.rem(s + k, NS), c)

    def at_crs(k):
        return (s, lax.rem(c + k, NC))

    barrier = pltpu.get_barrier_semaphore()
    for k in range(1, NS):
        pl.semaphore_signal(barrier, inc=1, device_id=at_str(k), device_id_type=MESH)
    for k in range(1, NC):
        pl.semaphore_signal(barrier, inc=1, device_id=at_crs(k), device_id_type=MESH)

    loads = [
        pltpu.make_async_copy(v_in, vn, in_sem.at[0]),
        pltpu.make_async_copy(series_in, sn, in_sem.at[1]),
        pltpu.make_async_copy(pattern_in, patn, in_sem.at[2]),
        pltpu.make_async_copy(mask_in, maskn, in_sem.at[3]),
        pltpu.make_async_copy(group_in, groupn, in_sem.at[4]),
        pltpu.make_async_copy(shunt_in, shn, in_sem.at[5]),
        pltpu.make_async_copy(photo_in, pn, in_sem.at[6]),
    ]
    quarter = pl.multiple_of((s // 4) * 128, 128)
    for k in range(NC):
        loads.append(
            pltpu.make_async_copy(
                inverse_in.at[:, pl.ds(pl.multiple_of(k * 512 + quarter, 128), 128)], staged.at[k], in_sem.at[7 + k]
            )
        )
    for copy in loads:
        copy.start()

    lane = lax.broadcasted_iota(jnp.int32, (ROWS, 128), 1)
    case_of = lane // 32
    is_first = lane == 0
    is_last = lane == 127
    case8 = case_of[0:8]
    sub8 = lax.broadcasted_iota(jnp.int32, (8, 128), 0)
    spot = (lax.broadcasted_iota(jnp.int32, (ROWS, 128), 0) == lane - 32 * case_of).astype(F32)

    def remote(src, dst, send, recv, who):
        return pltpu.make_async_remote_copy(
            src_ref=src, dst_ref=dst, send_sem=send, recv_sem=recv, device_id=who, device_id_type=MESH
        )

    def arrived(ref, sem):
        pltpu.make_async_copy(ref, ref, sem).wait()

    def rows_of(case, row):
        return pl.ds(case * FIELD + STEP + row, BLOCKS, stride=STEP)

    def edges_out(f, up, down, left, right):
        for case in range(CASES):
            up[case * 16 : case * 16 + 16, :] = f[rows_of(case, 0), :]
            down[case * 16 : case * 16 + 16, :] = f[rows_of(case, ROWS - 1), :]
        for block, ref in ((0, left), (BLOCKS - 1, right)):
            first = (block + 1) * STEP
            tile = jnp.concatenate(
                [f[case * FIELD + first : case * FIELD + first + ROWS, :] for case in range(CASES)], axis=0
            ).T
            ref[0:8, :] = tile[0:8] if block == 0 else tile[120:128]

    def edges_in(f, above, below, left, right):
        for case in range(CASES):
            f[rows_of(case, -1), :] = above[case * 16 : case * 16 + 16, :]
            f[rows_of(case, ROWS), :] = below[case * 16 : case * 16 + 16, :]
        for first, row in ((0, left[7:8, :]), (17 * STEP, right[0:1, :])):
            tile = jnp.broadcast_to(row, (128, 128)).T
            for case in range(CASES):
                f[case * FIELD + first : case * FIELD + first + ROWS, :] = tile[case * ROWS : case * ROWS + ROWS]

    def exchange(bufs, send, recv):
        up_s, down_s, left_s, right_s, above_r, below_r, left_r, right_r = bufs
        copies = [
            remote(up_s, below_r, send.at[0], recv.at[0], at_str(NS - 1)),
            remote(down_s, above_r, send.at[1], recv.at[1], at_str(1)),
            remote(left_s, right_r, send.at[2], recv.at[2], at_crs(NC - 1)),
            remote(right_s, left_r, send.at[3], recv.at[3], at_crs(1)),
        ]
        for copy in copies:
            copy.start()
        return copies

    def neighbours(f, case, base):
        def part(shift):
            return f[pl.ds(case * FIELD + base + shift, ROWS), :]

        here = part(0)
        right = jnp.where(is_last, pltpu.roll(part(STEP), 127, 1), pltpu.roll(here, 127, 1))
        left = jnp.where(is_first, pltpu.roll(part(-STEP), 1, 1), pltpu.roll(here, 1, 1))
        return here, part(1), part(-1), right, left

    def links(j, base):
        flat = pl.ds(pl.multiple_of(j * ROWS, ROWS), ROWS)
        return sf[pl.ds(base, ROWS), :], sf[pl.ds(base - 1, ROWS), :], rlf[flat, :], llf[flat, :]

    def jacobian(f, case, base, link):
        down, up, right_link, left_link = link
        here, below, above, right, left = neighbours(f, case, base)
        diagonal = dgf[pl.ds(case * FIELD + base, ROWS), :]
        return here, diagonal * here - down * below - up * above - right_link * right - left_link * left

    def fold(x):
        return x[0:8] + x[8:16] + x[16:24] + x[24:32]

    def by_case(parts):
        total = jnp.zeros((8, 128), F32)
        for case in range(CASES):
            total = jnp.where(case8 == case, jnp.sum(parts[case], axis=(0, 1), keepdims=True), total)
        return total

    def case_sums(x):
        total = jnp.zeros((8, 128), F32)
        for case in range(CASES):
            one = jnp.sum(jnp.where(case8 == case, x, 0.0), axis=1, keepdims=True)
            total = jnp.where(case8 == case, one, total)
        return total


    def spread(x, column, rows=ROWS):
        return jnp.broadcast_to(x[:, column : column + 1], (rows, 128))

    for copy in loads[:5]:
        copy.wait()
    level = jnp.zeros((ROWS, BLOCKS), F32)
    for number in range(4):
        level = level + jnp.where(patn[...] == number, F32(LEVELS[number]), F32(0.0))
    pk[...] = jnp.zeros_like(pk)
    pk[:, 0:16] = groupn[...].astype(F32)
    pk[:, 16:32] = level
    packed = pk[...]

    def lay_out(j, _):
        base = pl.multiple_of((j + 1) * STEP, 8)
        cols = pl.ds(pl.multiple_of(j * 128, 128), 128)
        for case in range(CASES):
            ef[pl.ds(case * FIELD + base, ROWS), :] = vn[case, :, cols]
        sf[pl.ds(base, ROWS), :] = sn[:, cols]
        return 0

    lax.fori_loop(0, BLOCKS, lay_out, 0)
    edges_out(ef, su_s, sd_s, sl_s, sr_s)
    su_s[64:72, :] = packed[0:8]
    sd_s[64:72, :] = packed[24:32]
    sd_s[72:88, :] = sf[pl.ds(STEP + ROWS - 1, BLOCKS, stride=STEP), :]
    sl_s[8:40, :] = packed
    sr_s[8:40, :] = packed

    pl.semaphore_wait(barrier, NS - 1 + NC - 1)
    setup_copies = exchange((su_s, sd_s, sl_s, sr_s, sd_r, su_r, sl_r, sr_r), setup_send, setup_recv)

    groups[...] = jnp.zeros_like(groups)
    half_mask = maskn[...].astype(F32) * 0.5
    for j in range(BLOCKS):
        base = (j + 1) * STEP
        group = spread(packed, j).astype(jnp.int32)
        groups[base : base + ROWS, :] = group
        low = group // 32
        code = (low % 16) * 8 + low // 16
        lb[j * ROWS : j * ROWS + ROWS, 0:128] = (lane == code).astype(F32).astype(BF16)
        dmf[j * ROWS : j * ROWS + ROWS, :] = spread(half_mask, j)
    for k in range(4):
        e_turn[:, k * 128 : k * 128 + 128] = lb[k * 128 : k * 128 + 128, 0:128].astype(F32).T.astype(BF16)

    same = lax.broadcasted_iota(jnp.int32, (128, 128), 0) // 32
    across = lax.broadcasted_iota(jnp.int32, (128, 128), 1) // 32
    block_ones = (same == across).astype(F32).astype(BF16)
    ones_pair[0:128, :] = block_ones
    ones_pair[128:256, :] = block_ones
    for case in range(CASES):
        wide = (same == case).astype(F32).astype(BF16)
        ones_wide[0:128, case * 128 : case * 128 + 128] = wide
        ones_wide[128:256, case * 128 : case * 128 + 128] = wide

    for copy in loads[7:]:
        copy.wait()

    def pick(i, _):
        rows = pl.ds(pl.multiple_of(i * 32, 32), 32)
        for side in range(2):
            block = jnp.zeros((ROWS, 128), F32)
            for k in range(4):
                turn = lax.rem(32 * k + 128 - 32 * lax.rem(s, 4), 128)
                block = jnp.where(case_of == k, pltpu.roll(staged[side * 4 + k, rows, :], turn, 1), block)
            high, low = halves(block)
            a_high[rows, side * 128 : side * 128 + 128] = high
            a_low[rows, side * 128 : side * 128 + 128] = low
        return 0

    lax.fori_loop(0, 16, pick, 0)
    for copy in loads[5:7]:
        copy.wait()


    for copy in setup_copies:
        copy.wait()
    edges_in(ef, sd_r, su_r, sl_r, sr_r)
    sf[pl.ds(STEP - 1, BLOCKS, stride=STEP), :] = sd_r[72:88, :]
    above8 = sd_r[64:72, :]
    below8 = su_r[64:72, :]
    for j in range(BLOCKS):
        base = (j + 1) * STEP
        groups[base - 1 : base, :] = spread(above8, j, 8)[7:8].astype(jnp.int32)
        groups[base + ROWS : base + ROWS + 1, :] = spread(below8, j, 8)[0:1].astype(jnp.int32)
    packed_left = sl_r[8:40, :]
    packed_right = sr_r[8:40, :]
    groups[0:ROWS, :] = spread(packed_left, BLOCKS - 1).astype(jnp.int32)
    groups[17 * STEP : 17 * STEP + ROWS, :] = spread(packed_right, 0).astype(jnp.int32)

    open_left = jnp.where(c == 0, 0.0, 1.0).astype(F32)
    open_right = jnp.where(c == NC - 1, 0.0, 1.0).astype(F32)
    row_levels = (
        [spread(packed_left, 16 + BLOCKS - 1)] + [spread(packed, 16 + j) for j in range(BLOCKS)] + [spread(packed_right, 16)]
    )
    for j in range(BLOCKS):
        here = row_levels[j + 1]
        right = jnp.minimum(here, row_levels[j + 2])
        left = jnp.minimum(here, row_levels[j])
        if j == BLOCKS - 1:
            right = right * open_right
        if j == 0:
            left = left * open_left
        rlf[j * ROWS : j * ROWS + ROWS, :] = jnp.where(is_last, right, here)
        llf[j * ROWS : j * ROWS + ROWS, :] = jnp.where(is_first, left, here)
        er[j * ROWS : j * ROWS + ROWS, :] = right
        el[j * ROWS : j * ROWS + ROWS, :] = left

    def block_columns(j, base, sums, target):
        total = jnp.zeros((ROWS, 128), F32)
        for case in range(CASES):
            total = jnp.where(case_of == case, jnp.sum(sums[case], axis=1, keepdims=True), total)
        if target is not None:
            target[pl.ds(pl.multiple_of(j * ROWS, ROWS), ROWS), :] = total
        return total

    def to_scatter(j, base, total):
        flat = pl.ds(pl.multiple_of(j * ROWS, ROWS), ROWS)
        high, low = halves(total * m_high[pl.ds(base, ROWS), :])
        lb[flat, 0:128] = high
        lb[flat, 128:256] = low

    def codes(i, _):
        rows = pl.ds(pl.multiple_of(i * 80, 16), 80)
        group = groups[rows, :]
        lanes = lax.broadcasted_iota(jnp.int32, (80, 128), 1)
        e_low[rows, :] = (lanes == group // 32).astype(F32).astype(BF16)
        m_high[rows, :] = (lanes % 32 == group % 32).astype(F32)
        return 0

    lax.fori_loop(0, FIELD // 80, codes, 0)

    def start_values(j, sums):
        base = pl.multiple_of((j + 1) * STEP, 8)
        cols = pl.ds(pl.multiple_of(j * 128, 128), 128)
        flat = pl.ds(pl.multiple_of(j * ROWS, ROWS), ROWS)
        link = links(j, base)
        down, up, right_link, left_link = link
        shunt = shn[:, cols]
        half = dmf[flat, :]
        edge = jnp.where(is_last, right_link, 0.0) + jnp.where(is_first, left_link, 0.0)
        out, rests, plain = [], [], []
        for case in range(CASES):
            at = pl.ds(case * FIELD + base, ROWS)
            here, below, above, right, left = neighbours(ef, case, base)
            slope = half * jnp.exp(here)
            ground = shunt + slope + down + up
            diagonal = ground + right_link + left_link
            rest = pn[case, :, cols] - (
                shunt * here
                + down * (here - below)
                + up * (here - above)
                + right_link * (here - right)
                + left_link * (here - left)
                + slope
                - half
            )
            inverse = 1.0 / diagonal
            dgf[at, :] = diagonal
            inf[at, :] = inverse
            rf[at, :] = rest
            scaled = rest * inverse
            qf[at, :] = scaled
            out.append(sums[case] + fold(rest * scaled))
            rests.append(rest)
            plain.append(ground + edge)
        block_columns(j, base, plain, sd)
        ss[flat, :] = jnp.broadcast_to(jnp.sum(down, axis=1, keepdims=True), (ROWS, 128))
        su[flat, :] = jnp.broadcast_to(jnp.sum(up, axis=1, keepdims=True), (ROWS, 128))
        to_scatter(j, base, block_columns(j, base, rests, None))
        return tuple(out)

    zero = jnp.zeros((8, 128), F32)
    start_sums = lax.fori_loop(0, BLOCKS, start_values, (zero,) * CASES)


    def send_restricted(k):
        out = dot(e_turn[...], lb[...])
        s1[k] = (out[:, 0:128] + out[:, 128:256]).reshape(NS, 8, 128)
        for off in range(1, NS):
            who = at_str(off)
            remote(s1.at[k, who[0]], r1.at[k, s], send_sem.at[k, 0], recv_sem.at[k, 0], who).start()
        r1[k, s] = s1[k, s]

    def send_chunk(k, scalars):
        arrived(r1.at[k, 0 : NS - 1], recv_sem.at[k, 0])
        s2[k, 0:8, :] = jnp.sum(r1[k], axis=0)
        s2[k, 8:16, :] = scalars
        for off in range(1, NC):
            remote(s2.at[k], r2.at[k, c], send_sem.at[k, 1], recv_sem.at[k, 1], at_crs(off)).start()
        r2[k, c] = s2[k]

    def send_product(k):
        arrived(r2.at[k, 0 : NC - 1], recv_sem.at[k, 1])
        total = jnp.sum(r2[k], axis=0)
        t = total[0:8]
        t_tile[...] = t
        placed = jnp.concatenate([jnp.broadcast_to(t[i : i + 1], (ROWS, 128)) * spot for i in range(NC)], axis=0)
        high, low = halves(placed)
        both = dot(jnp.concatenate([high, low], axis=0), ones_pair[0:128, :]).astype(BF16)
        right = jnp.concatenate([both[0:256], both[256:512]], axis=1)
        out = dot(a_high[...], right)
        out = out[:, 0:128] + out[:, 128:256] + dot(a_low[...], both[0:256])
        y = jnp.sum(out.reshape(16, ROWS, 128) * spot[None], axis=1)
        s3[k, 0:16, :] = y
        own = t_tile[pl.ds(c, 1), :]
        s3[k, 16:24, :] = jnp.where(sub8 == 0, jnp.broadcast_to(own, (8, 128)), total[8:16])
        for off in range(1, NS):
            remote(s3.at[k], r3.at[k, s], send_sem.at[k, 2], recv_sem.at[k, 2], at_str(off)).start()
        r3[k, s] = s3[k]

    RZ, RR, ALPHA, BETA, RQ, QQ = range(6)

    def row(x, i):
        return jnp.broadcast_to(x[i : i + 1], (8, 128))

    def send_correction(k):
        arrived(r3.at[k, 0 : NS - 1], recv_sem.at[k, 2])
        total = jnp.sum(r3[k], axis=0)
        y = total[0:16]
        t = jnp.concatenate([r3[k, i, 16:17, :] for i in range(NS)], axis=0)
        sums = total[16:24]
        if k == 0:
            state[RR] = row(sums, 1)
        else:
            alpha = state[RZ] / row(sums, 1)
            state[ALPHA] = alpha
            state[QQ] = row(sums, 2)
            state[RQ] = row(sums, 3)
            y = y_now[...] - alpha[0:1] * y
            t = t_now[...] - alpha[0:1] * t
        y_now[...] = y
        t_now[...] = t
        s4[k, 0:16, :] = y
        s4[k, 16:24, :] = jnp.broadcast_to(jnp.sum(y * t, axis=0, keepdims=True), (8, 128))
        for off in range(1, NC):
            remote(s4.at[k], r4.at[k, c], send_sem.at[k, 3], recv_sem.at[k, 3], at_crs(off)).start()
        r4[k, c] = s4[k]

    def to_cases(slot, x):
        for case in range(CASES):
            per_case[slot, case] = jnp.broadcast_to(x[:, case * 32 : case * 32 + 1], (8, 128))

    def receive_correction(k):
        arrived(r4.at[k, 0 : NC - 1], recv_sem.at[k, 3])
        correction = jnp.concatenate([r4[k, i, 0:16, :] for i in range(NC)], axis=0)
        high, low = halves(correction)
        picked = dot(e_low[...], jnp.concatenate([high, low], axis=1))
        mask = m_high[...]
        gm[:, 0:128] = (picked[:, 0:128] * mask).astype(BF16)
        gm[:, 128:256] = (picked[:, 128:256] * mask).astype(BF16)
        cb[...] = dot(gm[...], ones_pair[...])
        coarse = case_sums(jnp.sum(r4[k, :, 16:24, :], axis=0))
        if k == 0:
            state[RZ] = state[RR] + coarse
        else:
            alpha = state[ALPHA]
            smooth = state[RR] - 2.0 * alpha * state[RQ] + alpha * alpha * state[QQ]
            fresh = smooth + coarse
            state[RR] = smooth
            state[BETA] = fresh / state[RZ]
            state[RZ] = fresh
            to_cases(0, alpha)
            to_cases(1, state[BETA])

    def block_level(k):
        alpha = state[ALPHA][0:1]
        beta = state[BETA][0:1]

        def body(j, _):
            base = pl.multiple_of((j + 1) * STEP, 8)
            flat = pl.ds(pl.multiple_of(j * ROWS, ROWS), ROWS)
            value = bu[flat, :]
            if k:
                value = value - alpha * bw[flat, :]
                bu[flat, :] = value
                value = value + beta * bq[flat, :]
            value = (
                value
                + sd[flat, :] * cb[pl.ds(base, ROWS), :]
                - ss[flat, :] * cb[pl.ds(base + 1, ROWS), :]
                - su[flat, :] * cb[pl.ds(base - 1, ROWS), :]
                - er[flat, :] * cb[pl.ds(base + STEP, ROWS), :]
                - el[flat, :] * cb[pl.ds(base - STEP, ROWS), :]
            )
            bq[flat, :] = value
            to_scatter(j, base, value)
            return 0

        lax.fori_loop(0, BLOCKS, body, 0)


    def widen_correction():
        wide = dot(gm[...], ones_wide[...])
        for case in range(CASES):
            pcf[case * FIELD : case * FIELD + FIELD, :] = wide[:, case * 128 : case * 128 + 128]

    def next_direction(k):
        widen_correction()

        def body(j, sums):
            base = pl.multiple_of((j + 1) * STEP, 8)
            link = links(j, base)
            out = []
            for case in range(CASES):
                at = pl.ds(case * FIELD + base, ROWS)
                here, image = jacobian(pcf, case, base, link)
                rest = rf[at, :]
                inverse = inf[at, :]
                image = image + uf[at, :]
                if k:
                    alpha = per_case[0, case][0:1]
                    beta = per_case[1, case][0:1]
                    last_image = qf[at, :]
                    last_direction = df[at, :]
                    change = alpha * wf[at, :]
                    uf[at, :] = uf[at, :] - change
                    image = image - change + beta * last_image
                    rest = rest - alpha * last_image
                    rf[at, :] = rest
                    step = alpha * last_direction
                    xf[at, :] = step if k == 1 else xf[at, :] + step
                direction = rest * inverse + here
                if k:
                    direction = direction + beta * last_direction
                qf[at, :] = image
                df[at, :] = direction
                out.append(sums[3 * case] + fold(direction * image))
                if k < SOLVES - 1:
                    scaled = image * inverse
                    ef[at, :] = scaled
                    out.append(sums[3 * case + 1] + fold(image * scaled))
                    out.append(sums[3 * case + 2] + fold(rest * scaled))
                else:
                    out.extend([sums[3 * case + 1], sums[3 * case + 2]])
            return tuple(out)

        sums = lax.fori_loop(0, BLOCKS, body, (zero,) * (3 * CASES))
        tile = zero
        for kind in range(3 if k < SOLVES - 1 else 1):
            one = by_case([sums[3 * case + kind] for case in range(CASES)])
            tile = jnp.where(sub8 == kind + 1, one, tile)
        return tile

    def start_halo(k):
        edges_out(ef, hu_s.at[k], hd_s.at[k], hl_s.at[k], hr_s.at[k])
        bufs = [ref.at[k] for ref in (hu_s, hd_s, hl_s, hr_s, hd_r, hu_r, hl_r, hr_r)]
        return exchange(bufs, halo_send.at[k], halo_recv.at[k])

    def apply_scaled(k, copies, target, sums_to):
        for copy in copies:
            copy.wait()
        edges_in(ef, hd_r.at[k], hu_r.at[k], hl_r.at[k], hr_r.at[k])

        def body(j, _):
            base = pl.multiple_of((j + 1) * STEP, 8)
            link = links(j, base)
            values = []
            for case in range(CASES):
                _, image = jacobian(ef, case, base, link)
                target[pl.ds(case * FIELD + base, ROWS), :] = image
                values.append(image)
            block_columns(j, base, values, sums_to)
            return 0

        lax.fori_loop(0, BLOCKS, body, 0)


    send_restricted(0)

    def scaled_rest(j, _):
        base = pl.multiple_of((j + 1) * STEP, 8)
        for case in range(CASES):
            at = pl.ds(case * FIELD + base, ROWS)
            ef[at, :] = qf[at, :]
        return 0

    lax.fori_loop(0, BLOCKS, scaled_rest, 0)
    tile = jnp.where(sub8 == 1, by_case(start_sums), zero)
    copies = start_halo(0)
    send_chunk(0, tile)
    apply_scaled(0, copies, uf, bu)
    send_product(0)
    send_correction(0)
    receive_correction(0)
    for k in range(1, SOLVES):
        block_level(k - 1)
        send_restricted(k)
        tile = next_direction(k - 1)
        copies = start_halo(k)
        send_chunk(k, tile)
        send_product(k)
        apply_scaled(k, copies, wf, bw)
        send_correction(k)
        receive_correction(k)


    f1s[...] = next_direction(SOLVES - 1)
    for off in range(1, NS):
        remote(f1s, f1r.at[s], last_send.at[0], last_recv.at[0], at_str(off)).start()
    f1r[s] = f1s[...]
    arrived(f1r.at[0 : NS - 1], last_recv.at[0])
    f2s[...] = jnp.sum(f1r[...], axis=0)
    for off in range(1, NC):
        remote(f2s, f2r.at[c], last_send.at[1], last_recv.at[1], at_crs(off)).start()
    f2r[c] = f2s[...]
    arrived(f2r.at[0 : NC - 1], last_recv.at[1])
    alpha = state[RZ] / row(jnp.sum(f2r[...], axis=0), 1)
    to_cases(0, alpha)

    stores = []
    for case in range(CASES):

        def finish(j, _, case=case):
            base = pl.multiple_of((j + 1) * STEP, 8)
            cols = pl.ds(pl.multiple_of(j * 128, 128), 128)
            at = pl.ds(case * FIELD + base, ROWS)
            last = per_case[0, case][0:1]
            vn[case, :, cols] = xf[at, :] + last * df[at, :]
            pn[case, :, cols] = rf[at, :] - last * qf[at, :]
            return 0

        lax.fori_loop(0, BLOCKS, finish, 0)
        for number, (src, dst) in enumerate(((vn, step_out), (pn, rest_out))):
            copy = pltpu.make_async_copy(src.at[case], dst.at[case], out_sem.at[number, case])
            copy.start()
            stores.append(copy)


    for k in range(SOLVES):
        arrived(r1.at[k, 0 : NS - 1], send_sem.at[k, 0])
        arrived(r2.at[k, 0 : NC - 1], send_sem.at[k, 1])
        arrived(r3.at[k, 0 : NS - 1], send_sem.at[k, 2])
        arrived(r4.at[k, 0 : NC - 1], send_sem.at[k, 3])
    arrived(f1r.at[0 : NS - 1], last_send.at[0])
    arrived(f2r.at[0 : NC - 1], last_send.at[1])
    for copy in stores:
        copy.wait()


def shards(*args):
    field = (CASES * FIELD, 128)
    flat = (BLOCKS * ROWS, 128)

    def vmem(shape, dtype=F32):
        return pltpu.VMEM(shape, dtype)

    dma = pltpu.SemaphoreType.DMA
    scratch = [
        vmem((CASES, ROWS, 2048)), vmem((CASES, ROWS, 2048)), vmem((ROWS, 2048)), vmem((ROWS, 2048)),
        vmem((ROWS, BLOCKS), jnp.int32), vmem((ROWS, BLOCKS), jnp.int32), vmem((ROWS, BLOCKS), jnp.int32),
        vmem((NC, 512, 128)), vmem((512, 256), BF16), vmem((512, 256), BF16),
        *[vmem(field) for _ in range(10)],
        vmem((FIELD, 128)), vmem(flat), vmem(flat), vmem(flat),
        vmem((FIELD, 128)), vmem((FIELD, 256), BF16), vmem((FIELD, 128), BF16), vmem((FIELD, 128)),
        vmem((FIELD, 128), jnp.int32), vmem((128, 512), BF16), vmem((256, 128), BF16), vmem((256, 512), BF16),
        *[vmem(flat) for _ in range(8)], vmem((512, 256), BF16),
        vmem((ROWS, 128)),
        vmem((72, 128)), vmem((88, 128)), vmem((40, 128)), vmem((40, 128)),
        vmem((72, 128)), vmem((88, 128)), vmem((40, 128)), vmem((40, 128)),
        vmem((SOLVES, 64, 128)), vmem((SOLVES, 64, 128)), vmem((SOLVES, 8, 128)), vmem((SOLVES, 8, 128)),
        vmem((SOLVES, 64, 128)), vmem((SOLVES, 64, 128)), vmem((SOLVES, 8, 128)), vmem((SOLVES, 8, 128)),
        vmem((SOLVES, NS, 8, 128)), vmem((SOLVES, NS, 8, 128)),
        vmem((SOLVES, 16, 128)), vmem((SOLVES, NC, 16, 128)),
        vmem((SOLVES, 24, 128)), vmem((SOLVES, NS, 24, 128)),
        vmem((SOLVES, 24, 128)), vmem((SOLVES, NC, 24, 128)),
        vmem((8, 128)), vmem((NS, 8, 128)), vmem((8, 128)), vmem((NC, 8, 128)),
        vmem((16, 128)), vmem((16, 128)), vmem((8, 128)), vmem((6, 8, 128)), vmem((2, CASES, 8, 128)),
        dma((15,)), dma((2, CASES)), dma((4,)), dma((4,)), dma((SOLVES, 4)), dma((SOLVES, 4)),
        dma((SOLVES, 4)), dma((SOLVES, 4)), dma((2,)), dma((2,)),
    ]
    return pl.pallas_call(
        kernel,
        out_shape=[jax.ShapeDtypeStruct((CASES, ROWS, 2048), F32)] * 2,
        in_specs=[pl.BlockSpec(memory_space=pl.ANY)] * 8,
        out_specs=[pl.BlockSpec(memory_space=pl.ANY)] * 2,
        scratch_shapes=scratch,
        compiler_params=pltpu.CompilerParams(collective_id=0, has_side_effects=True, vmem_limit_bytes=50 * 2**20),
        name="newton",
    )(*args)


def solution(mesh):
    field = P(None, "str", "crs")
    plane = P("str", "crs")
    return jax.shard_map(
        shards,
        mesh=mesh,
        in_specs=(field, field, plane, plane, plane, plane, plane, P("crs", None)),
        out_specs=(field, field),
        check_vma=False,
    )
```

time: 1070 us -> 99.8 us (0.09)
  waiting for transfers between devices: 458 us -> 0 us
  blocking collectives: 435 us -> 0 us
  Pallas kernels: 0 us -> 91.4 us
  other arithmetic: 50.6 us -> 0 us
  starting transfers between devices: 36.8 us -> 0 us
  matrix products: 32.6 us -> 0 us
  local copies, waits for them, and re-layouts: 35 us -> 7.38 us
  between operations: 14.6 us -> 0.64 us
    psum x3 -> x0, waiting for transfers between devices: 453 us -> none  [coarse_solve(): total = lax.psum(incomplete_value, ('str', 'crs'))]
    psum x5 -> x0, blocking collectives: 351 us -> none  [the longest x3 209 us: precondition(): lax.psum(jnp.sum(remainder * smoothed, axis=(1, 2)), ('str', 'crs'))]
    pallas_call x0 -> x1, Pallas kernels: none -> 91.4 us  [shards(): pl.pallas_call(kernel, out_shape=[jax.ShapeDtypeStruct((CASES, ROWS, 2048...]
    all_gather x3 -> x0, blocking collectives: 83.9 us -> none  [coarse_solve(): correction = lax.all_gather(row_share, 'crs', axis=1, tiled=True)]
    ppermute x16 -> x0, starting transfers between devices: 36.2 us -> none  [the longest x8 20.1 us: with_halo(): lax.ppermute(lax.slice_in_dim(block, block.shape[dim] - width, None, axis...]
    dot_general x3 -> x0, matrix products: 32.6 us -> none  [coarse_solve(): lax.dot_general(total, coarse_inverse, (((1,), (1,)), ((), ())), precisio...]
    scatter-add x3 -> x0, other arithmetic: 11.6 us -> none  [restrict(): jax.ops.segment_sum(block_sums.T, flat_groups, num_segments=coarse_count)]
    reshape x6 -> x0, local copies, waits for them, and re-layouts: 10.9 us -> none  [the longest x3 5.88 us: widen(): return spread.reshape(shape[:-1] + (shape[-1] * 128,))]
  transfers between devices with their start and end apart: 19 -> 0, of which waited for: 9 -> 0; matrix products, arithmetic and copies ran while one was open for 0% -> 0% of each run, Pallas kernels for 0% -> 0%
where the time goes in v1:
time: 99.8 us; the launch traced here: 99.5 us
  Pallas kernels  91.4 us (92%)
  local copies, waits for them, and re-layouts  7.38 us (7%)
    pallas_call x1, Pallas kernels, shards(): pl.pallas_call(kernel, out_shape=[jax.ShapeDtypeStruct((CASES, ROWS, 2048...  91.4 us
    unnamed x11, local copies, waits for them, and re-layouts  7.38 us

profile of v1, /device:TPU:1, one launch (start us, length us, event | category | flops | bytes accessed | tf_op | source)
XLA Modules:
  0.0 99.5 jit_solution(8244957280414968370)
XLA Ops:
  0.6 0.8 copy.10.pattern_in
  1.4 0.8 copy.11.mask_in
  2.2 0.8 copy.12.group_in
  2.9 0.0 copy-start
  2.9 1.2 %copy-done = f32[4,32,2048]{2,1,0:T(8,128)S(1)} copy-done((f32[4,32,2048]{2,1,0:T(8,128)S(1)}, f32[4,32,2048]{2,1,0:T(8,128)}, u32[]{:S(2)}) %copy-start) | copy-done | bytes 1048600
  4.2 0.0 copy-start.1
  4.2 0.9 copy-done.1
  5.1 0.0 copy-start.2
  5.1 0.9 copy-done.2
  6.1 91.4 %newton.1 = (f32[4,32,2048]{2,1,0:T(8,128)S(1)}, f32[4,32,2048]{2,1,0:T(8,128)S(1)}) custom-call(f32[4,32,2048]{2,1,0:T(8,128)S(1)} %copy-done, f32[4,32,2048]{2,1,0:T(8,128)} %photo_in.1, f32[32,2048]{1,0:T(8,128)S(1)} %copy-done.1, f32[32,2048]{1,0:T(8,128)S(1)} %copy-done.2, s32[32,16]{1,0:T(8,128)S(1)} %copy.10.pattern_in, s32[32,16]{1,0:T(8,128)S(1)} %copy.11.mask_in, ...), custom_call_target="tpu_custom_call" | custom-call | tf_op jit(solution)/shard_map/newton/pallas_call | solution.py:638
  97.5 1.0 copy.15
  98.5 1.0 copy.16
Async XLA Ops:
  2.9 1.2 %copy-start = (f32[4,32,2048]{2,1,0:T(8,128)S(1)}, f32[4,32,2048]{2,1,0:T(8,128)}, u32[]{:S(2)}) copy-start(f32[4,32,2048]{2,1,0:T(8,128)} %v_in.1) | copy-start | bytes 3145732
  4.2 0.9 copy-start.1
  5.1 0.9 copy-start.2

commit v2 on v1

--- a/solution.py
+++ b/solution.py
@@ -1,3 +1,5 @@
+import itertools
+
 import jax
 import jax.numpy as jnp
 from jax import lax
@@ -31,17 +33,17 @@
 
 def kernel(
     v_in, photo_in, shunt_in, series_in, pattern_in, mask_in, group_in, inverse_in,
-    step_out, rest_out,
+    xf_out, df_out, rf_out, qf_out, alpha_out,
     vn, pn, shn, sn, patn, maskn, groupn, staged, a_high, a_low,
     ef, rf, qf, df, xf, uf, wf, dgf, inf, pcf,
     sf, rlf, llf, dmf,
     cb, gm, e_low, m_high, groups, e_turn, ones_pair, ones_wide,
     bu, bw, bq, sd, ss, su, er, el, lb,
-    pk, su_s, sd_s, sl_s, sr_s, su_r, sd_r, sl_r, sr_r,
+    pk, turned, su_s, sd_s, sl_s, sr_s, su_r, sd_r, sl_r, sr_r,
     hu_s, hd_s, hl_s, hr_s, hu_r, hd_r, hl_r, hr_r,
-    s1, r1, s2, r2, s3, r3, s4, r4, f1s, f1r, f2s, f2r,
-    y_now, t_now, t_tile, state, per_case,
-    in_sem, out_sem, setup_send, setup_recv, halo_send, halo_recv, send_sem, recv_sem, last_send, last_recv,
+    s1, r1, s2, r2, s3, r3, s4, r4, fs, fr,
+    y_now, t_now, t_tile, state, per_case, local,
+    in_sem, setup_send, setup_recv, halo_send, halo_recv, send_sem, recv_sem, last_send, last_recv,
 ):
     s = lax.axis_index("str")
     c = lax.axis_index("crs")
@@ -52,11 +54,28 @@
     def at_crs(k):
         return (s, lax.rem(c + k, NC))
 
+    str_at = {}
+    for key in itertools.product(range(2), range(4), range(2)):
+        x_lo, y, core = (lax.rem(p + k, n) for p, k, n in zip((s // 8, lax.rem(s // 2, 4), lax.rem(s, 2)), key, (2, 4, 2)))
+        str_at[key] = (x_lo * 4 + y) * 2 + core
+    crs_at = {}
+    for key in itertools.product(range(2), range(4)):
+        x_hi, z = (lax.rem(p + k, n) for p, k, n in zip((c // 4, lax.rem(c, 4)), key, (2, 4)))
+        crs_at[key] = x_hi * 4 + z
+
+    def far_first(key):
+        x_lo, y, core, x_hi, z = key
+        across = 1 if x_lo else 2 * x_hi
+        return -(across + min(y, 4 - y) + min(z, 4 - z) + 0.5 * core)
+
+    everyone = sorted(itertools.product(range(2), range(4), range(2), range(2), range(4)), key=far_first)[:-1]
+    everyone = [(key, (str_at[key[:3]], crs_at[key[3:]])) for key in everyone]
+    str_peers = [(who[0], c) for key, who in everyone if key[3:] == (0, 0)]
+    crs_peers = [(s, who[1]) for key, who in everyone if key[:3] == (0, 0, 0)]
+
     barrier = pltpu.get_barrier_semaphore()
-    for k in range(1, NS):
-        pl.semaphore_signal(barrier, inc=1, device_id=at_str(k), device_id_type=MESH)
-    for k in range(1, NC):
-        pl.semaphore_signal(barrier, inc=1, device_id=at_crs(k), device_id_type=MESH)
+    for who in str_peers + crs_peers:
+        pl.semaphore_signal(barrier, inc=1, device_id=who, device_id_type=MESH)
 
     loads = [
         pltpu.make_async_copy(v_in, vn, in_sem.at[0]),
@@ -133,8 +152,8 @@
             return f[pl.ds(case * FIELD + base + shift, ROWS), :]
 
         here = part(0)
-        right = jnp.where(is_last, pltpu.roll(part(STEP), 127, 1), pltpu.roll(here, 127, 1))
-        left = jnp.where(is_first, pltpu.roll(part(-STEP), 1, 1), pltpu.roll(here, 1, 1))
+        right = pltpu.roll(jnp.where(is_first, part(STEP), here), 127, 1)
+        left = pltpu.roll(jnp.where(is_last, part(-STEP), here), 1, 1)
         return here, part(1), part(-1), right, left
 
     def links(j, base):
@@ -169,12 +188,14 @@
 
     for copy in loads[:5]:
         copy.wait()
-    level = jnp.zeros((ROWS, BLOCKS), F32)
+    level = jnp.zeros((BLOCKS, ROWS), F32)
     for number in range(4):
         level = level + jnp.where(patn[...] == number, F32(LEVELS[number]), F32(0.0))
-    pk[...] = jnp.zeros_like(pk)
-    pk[:, 0:16] = groupn[...].astype(F32)
-    pk[:, 16:32] = level
+    turned[...] = jnp.zeros_like(turned)
+    turned[0:16, 0:32] = groupn[...].astype(F32)
+    turned[16:32, 0:32] = level
+    turned[32:48, 0:32] = maskn[...].astype(F32) * 0.5
+    pk[...] = turned[...].T[0:ROWS]
     packed = pk[...]
 
     def lay_out(j, _):
@@ -190,14 +211,15 @@
     su_s[64:72, :] = packed[0:8]
     sd_s[64:72, :] = packed[24:32]
     sd_s[72:88, :] = sf[pl.ds(STEP + ROWS - 1, BLOCKS, stride=STEP), :]
-    sl_s[8:40, :] = packed
-    sr_s[8:40, :] = packed
+    sl_s[1:2, :] = turned[0:1, :]
+    sl_s[2:3, :] = turned[16:17, :]
+    sr_s[1:2, :] = turned[15:16, :]
+    sr_s[2:3, :] = turned[31:32, :]
 
     pl.semaphore_wait(barrier, NS - 1 + NC - 1)
     setup_copies = exchange((su_s, sd_s, sl_s, sr_s, sd_r, su_r, sl_r, sr_r), setup_send, setup_recv)
 
     groups[...] = jnp.zeros_like(groups)
-    half_mask = maskn[...].astype(F32) * 0.5
     for j in range(BLOCKS):
         base = (j + 1) * STEP
         group = spread(packed, j).astype(jnp.int32)
@@ -205,7 +227,7 @@
         low = group // 32
         code = (low % 16) * 8 + low // 16
         lb[j * ROWS : j * ROWS + ROWS, 0:128] = (lane == code).astype(F32).astype(BF16)
-        dmf[j * ROWS : j * ROWS + ROWS, :] = spread(half_mask, j)
+        dmf[j * ROWS : j * ROWS + ROWS, :] = spread(packed, 32 + j)
     for k in range(4):
         e_turn[:, k * 128 : k * 128 + 128] = lb[k * 128 : k * 128 + 128, 0:128].astype(F32).T.astype(BF16)
 
@@ -249,15 +271,17 @@
         base = (j + 1) * STEP
         groups[base - 1 : base, :] = spread(above8, j, 8)[7:8].astype(jnp.int32)
         groups[base + ROWS : base + ROWS + 1, :] = spread(below8, j, 8)[0:1].astype(jnp.int32)
-    packed_left = sl_r[8:40, :]
-    packed_right = sr_r[8:40, :]
-    groups[0:ROWS, :] = spread(packed_left, BLOCKS - 1).astype(jnp.int32)
-    groups[17 * STEP : 17 * STEP + ROWS, :] = spread(packed_right, 0).astype(jnp.int32)
+    packed_left = jnp.broadcast_to(sl_r[1:2, :], (128, 128)).T[0:ROWS]
+    packed_right = jnp.broadcast_to(sr_r[1:2, :], (128, 128)).T[0:ROWS]
+    groups[0:ROWS, :] = packed_left.astype(jnp.int32)
+    groups[17 * STEP : 17 * STEP + ROWS, :] = packed_right.astype(jnp.int32)
+    level_left = jnp.broadcast_to(sl_r[2:3, :], (128, 128)).T[0:ROWS]
+    level_right = jnp.broadcast_to(sr_r[2:3, :], (128, 128)).T[0:ROWS]
 
     open_left = jnp.where(c == 0, 0.0, 1.0).astype(F32)
     open_right = jnp.where(c == NC - 1, 0.0, 1.0).astype(F32)
     row_levels = (
-        [spread(packed_left, 16 + BLOCKS - 1)] + [spread(packed, 16 + j) for j in range(BLOCKS)] + [spread(packed_right, 16)]
+        [level_left] + [spread(packed, 16 + j) for j in range(BLOCKS)] + [level_right]
     )
     for j in range(BLOCKS):
         here = row_levels[j + 1]
@@ -296,22 +320,18 @@
 
     lax.fori_loop(0, FIELD // 80, codes, 0)
 
-    def start_values(j, sums):
+    def start_rest(j, _):
         base = pl.multiple_of((j + 1) * STEP, 8)
         cols = pl.ds(pl.multiple_of(j * 128, 128), 128)
         flat = pl.ds(pl.multiple_of(j * ROWS, ROWS), ROWS)
-        link = links(j, base)
-        down, up, right_link, left_link = link
+        down, up, right_link, left_link = links(j, base)
         shunt = shn[:, cols]
         half = dmf[flat, :]
-        edge = jnp.where(is_last, right_link, 0.0) + jnp.where(is_first, left_link, 0.0)
-        out, rests, plain = [], [], []
+        rests = []
         for case in range(CASES):
             at = pl.ds(case * FIELD + base, ROWS)
             here, below, above, right, left = neighbours(ef, case, base)
             slope = half * jnp.exp(here)
-            ground = shunt + slope + down + up
-            diagonal = ground + right_link + left_link
             rest = pn[case, :, cols] - (
                 shunt * here
                 + down * (here - below)
@@ -321,30 +341,45 @@
                 + slope
                 - half
             )
+            dgf[at, :] = slope
+            rf[at, :] = rest
+            rests.append(rest)
+        to_scatter(j, base, block_columns(j, base, rests, None))
+        return 0
+
+    def start_scaled(j, sums):
+        base = pl.multiple_of((j + 1) * STEP, 8)
+        cols = pl.ds(pl.multiple_of(j * 128, 128), 128)
+        flat = pl.ds(pl.multiple_of(j * ROWS, ROWS), ROWS)
+        down, up, right_link, left_link = links(j, base)
+        shunt = shn[:, cols]
+        edge = jnp.where(is_last, right_link, 0.0) + jnp.where(is_first, left_link, 0.0)
+        out, plain = [], []
+        for case in range(CASES):
+            at = pl.ds(case * FIELD + base, ROWS)
+            ground = shunt + dgf[at, :] + down + up
+            diagonal = ground + right_link + left_link
             inverse = 1.0 / diagonal
+            rest = rf[at, :]
+            scaled = rest * inverse
             dgf[at, :] = diagonal
             inf[at, :] = inverse
-            rf[at, :] = rest
-            scaled = rest * inverse
-            qf[at, :] = scaled
+            ef[at, :] = scaled
             out.append(sums[case] + fold(rest * scaled))
-            rests.append(rest)
             plain.append(ground + edge)
         block_columns(j, base, plain, sd)
         ss[flat, :] = jnp.broadcast_to(jnp.sum(down, axis=1, keepdims=True), (ROWS, 128))
         su[flat, :] = jnp.broadcast_to(jnp.sum(up, axis=1, keepdims=True), (ROWS, 128))
-        to_scatter(j, base, block_columns(j, base, rests, None))
         return tuple(out)
 
     zero = jnp.zeros((8, 128), F32)
-    start_sums = lax.fori_loop(0, BLOCKS, start_values, (zero,) * CASES)
+    lax.fori_loop(0, BLOCKS, start_rest, 0)
 
 
     def send_restricted(k):
         out = dot(e_turn[...], lb[...])
         s1[k] = (out[:, 0:128] + out[:, 128:256]).reshape(NS, 8, 128)
-        for off in range(1, NS):
-            who = at_str(off)
+        for who in str_peers:
             remote(s1.at[k, who[0]], r1.at[k, s], send_sem.at[k, 0], recv_sem.at[k, 0], who).start()
         r1[k, s] = s1[k, s]
 
@@ -352,8 +387,8 @@
         arrived(r1.at[k, 0 : NS - 1], recv_sem.at[k, 0])
         s2[k, 0:8, :] = jnp.sum(r1[k], axis=0)
         s2[k, 8:16, :] = scalars
-        for off in range(1, NC):
-            remote(s2.at[k], r2.at[k, c], send_sem.at[k, 1], recv_sem.at[k, 1], at_crs(off)).start()
+        for who in crs_peers:
+            remote(s2.at[k], r2.at[k, c], send_sem.at[k, 1], recv_sem.at[k, 1], who).start()
         r2[k, c] = s2[k]
 
     def send_product(k):
@@ -371,8 +406,8 @@
         s3[k, 0:16, :] = y
         own = t_tile[pl.ds(c, 1), :]
         s3[k, 16:24, :] = jnp.where(sub8 == 0, jnp.broadcast_to(own, (8, 128)), total[8:16])
-        for off in range(1, NS):
-            remote(s3.at[k], r3.at[k, s], send_sem.at[k, 2], recv_sem.at[k, 2], at_str(off)).start()
+        for who in str_peers:
+            remote(s3.at[k], r3.at[k, s], send_sem.at[k, 2], recv_sem.at[k, 2], who).start()
         r3[k, s] = s3[k]
 
     RZ, RR, ALPHA, BETA, RQ, QQ = range(6)
@@ -399,8 +434,8 @@
         t_now[...] = t
         s4[k, 0:16, :] = y
         s4[k, 16:24, :] = jnp.broadcast_to(jnp.sum(y * t, axis=0, keepdims=True), (8, 128))
-        for off in range(1, NC):
-            remote(s4.at[k], r4.at[k, c], send_sem.at[k, 3], recv_sem.at[k, 3], at_crs(off)).start()
+        for who in crs_peers:
+            remote(s4.at[k], r4.at[k, c], send_sem.at[k, 3], recv_sem.at[k, 3], who).start()
         r4[k, c] = s4[k]
 
     def to_cases(slot, x):
@@ -432,28 +467,33 @@
     def block_level(k):
         alpha = state[ALPHA][0:1]
         beta = state[BETA][0:1]
-
-        def body(j, _):
+        final = k == SOLVES - 1
+
+        def body(j, energy):
             base = pl.multiple_of((j + 1) * STEP, 8)
             flat = pl.ds(pl.multiple_of(j * ROWS, ROWS), ROWS)
             value = bu[flat, :]
             if k:
                 value = value - alpha * bw[flat, :]
-                bu[flat, :] = value
+                if not final:
+                    bu[flat, :] = value
                 value = value + beta * bq[flat, :]
-            value = (
-                value
-                + sd[flat, :] * cb[pl.ds(base, ROWS), :]
+            here = cb[pl.ds(base, ROWS), :]
+            stencil = (
+                sd[flat, :] * here
                 - ss[flat, :] * cb[pl.ds(base + 1, ROWS), :]
                 - su[flat, :] * cb[pl.ds(base - 1, ROWS), :]
                 - er[flat, :] * cb[pl.ds(base + STEP, ROWS), :]
                 - el[flat, :] * cb[pl.ds(base - STEP, ROWS), :]
             )
+            if final:
+                return energy + fold(here * (stencil + 2.0 * value))
+            value = value + stencil
             bq[flat, :] = value
             to_scatter(j, base, value)
-            return 0
-
-        lax.fori_loop(0, BLOCKS, body, 0)
+            return energy
+
+        return lax.fori_loop(0, BLOCKS, body, zero)
 
 
     def widen_correction():
@@ -463,9 +503,12 @@
 
     def next_direction(k):
         widen_correction()
+        final = k == SOLVES - 1
+        kinds = {0: 3, SOLVES - 2: 5, SOLVES - 1: 0}[k]
 
         def body(j, sums):
             base = pl.multiple_of((j + 1) * STEP, 8)
+            cols = pl.ds(pl.multiple_of(j * 128, 128), 128)
             link = links(j, base)
             out = []
             for case in range(CASES):
@@ -473,38 +516,44 @@
                 here, image = jacobian(pcf, case, base, link)
                 rest = rf[at, :]
                 inverse = inf[at, :]
-                image = image + uf[at, :]
+                smooth = uf[at, :]
                 if k:
                     alpha = per_case[0, case][0:1]
                     beta = per_case[1, case][0:1]
                     last_image = qf[at, :]
                     last_direction = df[at, :]
-                    change = alpha * wf[at, :]
-                    uf[at, :] = uf[at, :] - change
-                    image = image - change + beta * last_image
+                    smooth = smooth - alpha * wf[at, :]
+                    image = image + beta * last_image
                     rest = rest - alpha * last_image
-                    rf[at, :] = rest
                     step = alpha * last_direction
-                    xf[at, :] = step if k == 1 else xf[at, :] + step
+                    if k > 1:
+                        step = step + xf[at, :]
+                image = image + smooth
                 direction = rest * inverse + here
                 if k:
                     direction = direction + beta * last_direction
+                if final:
+                    xf_out[case, :, cols] = step
+                    rf_out[case, :, cols] = rest
+                    df_out[case, :, cols] = direction
+                    qf_out[case, :, cols] = image
+                    continue
+                if k:
+                    uf[at, :] = smooth
+                    rf[at, :] = rest
+                    xf[at, :] = step
                 qf[at, :] = image
                 df[at, :] = direction
-                out.append(sums[3 * case] + fold(direction * image))
-                if k < SOLVES - 1:
-                    scaled = image * inverse
-                    ef[at, :] = scaled
-                    out.append(sums[3 * case + 1] + fold(image * scaled))
-                    out.append(sums[3 * case + 2] + fold(rest * scaled))
-                else:
-                    out.extend([sums[3 * case + 1], sums[3 * case + 2]])
+                scaled = image * inverse
+                ef[at, :] = scaled
+                terms = [direction * image, image * scaled, rest * scaled, rest * inverse * smooth, scaled * smooth]
+                out.extend(sums[kinds * case + i] + fold(terms[i]) for i in range(kinds))
             return tuple(out)
 
-        sums = lax.fori_loop(0, BLOCKS, body, (zero,) * (3 * CASES))
+        sums = lax.fori_loop(0, BLOCKS, body, (zero,) * (kinds * CASES))
         tile = zero
-        for kind in range(3 if k < SOLVES - 1 else 1):
-            one = by_case([sums[3 * case + kind] for case in range(CASES)])
+        for kind in range(kinds):
+            one = by_case([sums[kinds * case + kind] for case in range(CASES)])
             tile = jnp.where(sub8 == kind + 1, one, tile)
         return tile
 
@@ -518,30 +567,24 @@
             copy.wait()
         edges_in(ef, hd_r.at[k], hu_r.at[k], hl_r.at[k], hr_r.at[k])
 
-        def body(j, _):
+        def body(j, sums):
             base = pl.multiple_of((j + 1) * STEP, 8)
             link = links(j, base)
-            values = []
+            values, out = [], []
             for case in range(CASES):
-                _, image = jacobian(ef, case, base, link)
+                here, image = jacobian(ef, case, base, link)
                 target[pl.ds(case * FIELD + base, ROWS), :] = image
                 values.append(image)
+                if k == SOLVES - 1:
+                    out.append(sums[case] + fold(here * image))
             block_columns(j, base, values, sums_to)
-            return 0
-
-        lax.fori_loop(0, BLOCKS, body, 0)
+            return tuple(out)
+
+        return lax.fori_loop(0, BLOCKS, body, (zero,) * (CASES if k == SOLVES - 1 else 0))
 
 
     send_restricted(0)
-
-    def scaled_rest(j, _):
-        base = pl.multiple_of((j + 1) * STEP, 8)
-        for case in range(CASES):
-            at = pl.ds(case * FIELD + base, ROWS)
-            ef[at, :] = qf[at, :]
-        return 0
-
-    lax.fori_loop(0, BLOCKS, scaled_rest, 0)
+    start_sums = lax.fori_loop(0, BLOCKS, start_scaled, (zero,) * CASES)
     tile = jnp.where(sub8 == 1, by_case(start_sums), zero)
     copies = start_halo(0)
     send_chunk(0, tile)
@@ -553,44 +596,36 @@
         block_level(k - 1)
         send_restricted(k)
         tile = next_direction(k - 1)
+        if k == SOLVES - 1:
+            local[...] = tile
         copies = start_halo(k)
         send_chunk(k, tile)
         send_product(k)
-        apply_scaled(k, copies, wf, bw)
+        scaled_sums = apply_scaled(k, copies, wf, bw)
         send_correction(k)
         receive_correction(k)
 
 
-    f1s[...] = next_direction(SOLVES - 1)
-    for off in range(1, NS):
-        remote(f1s, f1r.at[s], last_send.at[0], last_recv.at[0], at_str(off)).start()
-    f1r[s] = f1s[...]
-    arrived(f1r.at[0 : NS - 1], last_recv.at[0])
-    f2s[...] = jnp.sum(f1r[...], axis=0)
-    for off in range(1, NC):
-        remote(f2s, f2r.at[c], last_send.at[1], last_recv.at[1], at_crs(off)).start()
-    f2r[c] = f2s[...]
-    arrived(f2r.at[0 : NC - 1], last_recv.at[1])
-    alpha = state[RZ] / row(jnp.sum(f2r[...], axis=0), 1)
-    to_cases(0, alpha)
-
-    stores = []
+    alpha = state[ALPHA]
+    beta = state[BETA]
+    energy = jnp.sum(block_level(SOLVES - 1), axis=0, keepdims=True)
+    dq, qq, rq, eu, qu = (row(local[...], i) for i in range(1, 6))
+    energy = (
+        energy
+        + (eu - 2.0 * alpha * qu + alpha * alpha * by_case(scaled_sums))
+        + 2.0 * beta * (rq - alpha * qq)
+        + beta * beta * dq
+    )
+    here = s * NC + c
+    fs[...] = energy[0:1]
+    for _, who in everyone:
+        remote(fs, fr.at[here], last_send.at[0], last_recv.at[0], who).start()
+    fr[here] = fs[...]
+    next_direction(SOLVES - 1)
+    arrived(fr.at[0 : NS * NC - 1], last_recv.at[0])
+    alpha = state[RZ] / jnp.broadcast_to(jnp.sum(fr[...], axis=0), (8, 128))
     for case in range(CASES):
-
-        def finish(j, _, case=case):
-            base = pl.multiple_of((j + 1) * STEP, 8)
-            cols = pl.ds(pl.multiple_of(j * 128, 128), 128)
-            at = pl.ds(case * FIELD + base, ROWS)
-            last = per_case[0, case][0:1]
-            vn[case, :, cols] = xf[at, :] + last * df[at, :]
-            pn[case, :, cols] = rf[at, :] - last * qf[at, :]
-            return 0
-
-        lax.fori_loop(0, BLOCKS, finish, 0)
-        for number, (src, dst) in enumerate(((vn, step_out), (pn, rest_out))):
-            copy = pltpu.make_async_copy(src.at[case], dst.at[case], out_sem.at[number, case])
-            copy.start()
-            stores.append(copy)
+        alpha_out[case : case + 1, :] = jnp.broadcast_to(alpha[0:1, case * 32 : case * 32 + 1], (1, 2048))
 
 
     for k in range(SOLVES):
@@ -598,13 +633,10 @@
         arrived(r2.at[k, 0 : NC - 1], send_sem.at[k, 1])
         arrived(r3.at[k, 0 : NS - 1], send_sem.at[k, 2])
         arrived(r4.at[k, 0 : NC - 1], send_sem.at[k, 3])
-    arrived(f1r.at[0 : NS - 1], last_send.at[0])
-    arrived(f2r.at[0 : NC - 1], last_send.at[1])
-    for copy in stores:
-        copy.wait()
-
-
-def shards(*args):
+    arrived(fr.at[0 : NS * NC - 1], last_send.at[0])
+
+
+def shards(voltage, photocurrent, shunt, series, pattern, diode_mask, aggregate, coarse_inverse):
     field = (CASES * FIELD, 128)
     flat = (BLOCKS * ROWS, 128)
 
@@ -614,36 +646,39 @@
     dma = pltpu.SemaphoreType.DMA
     scratch = [
         vmem((CASES, ROWS, 2048)), vmem((CASES, ROWS, 2048)), vmem((ROWS, 2048)), vmem((ROWS, 2048)),
-        vmem((ROWS, BLOCKS), jnp.int32), vmem((ROWS, BLOCKS), jnp.int32), vmem((ROWS, BLOCKS), jnp.int32),
+        vmem((BLOCKS, ROWS), jnp.int32), vmem((BLOCKS, ROWS), jnp.int32), vmem((BLOCKS, ROWS), jnp.int32),
         vmem((NC, 512, 128)), vmem((512, 256), BF16), vmem((512, 256), BF16),
         *[vmem(field) for _ in range(10)],
         vmem((FIELD, 128)), vmem(flat), vmem(flat), vmem(flat),
         vmem((FIELD, 128)), vmem((FIELD, 256), BF16), vmem((FIELD, 128), BF16), vmem((FIELD, 128)),
         vmem((FIELD, 128), jnp.int32), vmem((128, 512), BF16), vmem((256, 128), BF16), vmem((256, 512), BF16),
         *[vmem(flat) for _ in range(8)], vmem((512, 256), BF16),
-        vmem((ROWS, 128)),
-        vmem((72, 128)), vmem((88, 128)), vmem((40, 128)), vmem((40, 128)),
-        vmem((72, 128)), vmem((88, 128)), vmem((40, 128)), vmem((40, 128)),
+        vmem((ROWS, 128)), vmem((128, 128)),
+        vmem((72, 128)), vmem((88, 128)), vmem((8, 128)), vmem((8, 128)),
+        vmem((72, 128)), vmem((88, 128)), vmem((8, 128)), vmem((8, 128)),
         vmem((SOLVES, 64, 128)), vmem((SOLVES, 64, 128)), vmem((SOLVES, 8, 128)), vmem((SOLVES, 8, 128)),
         vmem((SOLVES, 64, 128)), vmem((SOLVES, 64, 128)), vmem((SOLVES, 8, 128)), vmem((SOLVES, 8, 128)),
         vmem((SOLVES, NS, 8, 128)), vmem((SOLVES, NS, 8, 128)),
         vmem((SOLVES, 16, 128)), vmem((SOLVES, NC, 16, 128)),
         vmem((SOLVES, 24, 128)), vmem((SOLVES, NS, 24, 128)),
         vmem((SOLVES, 24, 128)), vmem((SOLVES, NC, 24, 128)),
-        vmem((8, 128)), vmem((NS, 8, 128)), vmem((8, 128)), vmem((NC, 8, 128)),
-        vmem((16, 128)), vmem((16, 128)), vmem((8, 128)), vmem((6, 8, 128)), vmem((2, CASES, 8, 128)),
-        dma((15,)), dma((2, CASES)), dma((4,)), dma((4,)), dma((SOLVES, 4)), dma((SOLVES, 4)),
-        dma((SOLVES, 4)), dma((SOLVES, 4)), dma((2,)), dma((2,)),
+        vmem((1, 128)), vmem((NS * NC, 1, 128)),
+        vmem((16, 128)), vmem((16, 128)), vmem((8, 128)), vmem((6, 8, 128)), vmem((2, CASES, 8, 128)), vmem((8, 128)),
+        dma((15,)), dma((4,)), dma((4,)), dma((SOLVES, 4)), dma((SOLVES, 4)),
+        dma((SOLVES, 4)), dma((SOLVES, 4)), dma((1,)), dma((1,)),
     ]
-    return pl.pallas_call(
+    tall = jax.ShapeDtypeStruct((CASES, ROWS, 2048), F32)
+    step, direction, rest, image, alpha = pl.pallas_call(
         kernel,
-        out_shape=[jax.ShapeDtypeStruct((CASES, ROWS, 2048), F32)] * 2,
-        in_specs=[pl.BlockSpec(memory_space=pl.ANY)] * 8,
-        out_specs=[pl.BlockSpec(memory_space=pl.ANY)] * 2,
+        out_shape=[tall] * 4 + [jax.ShapeDtypeStruct((CASES, 2048), F32)],
+        in_specs=[pl.BlockSpec(memory_space=pltpu.HBM)] * 8,
+        out_specs=[pl.BlockSpec(memory_space=pltpu.VMEM)] * 5,
         scratch_shapes=scratch,
-        compiler_params=pltpu.CompilerParams(collective_id=0, has_side_effects=True, vmem_limit_bytes=50 * 2**20),
+        compiler_params=pltpu.CompilerParams(collective_id=0, has_side_effects=True, vmem_limit_bytes=54 * 2**20),
         name="newton",
-    )(*args)
+    )(voltage, photocurrent, shunt, series, pattern.T, diode_mask.T, aggregate.T, coarse_inverse)
+    alpha = alpha[:, None, :]
+    return step + alpha * direction, rest - alpha * image
 
 
 def solution(mesh):

time: 99.8 us -> 90.5 us (0.907)
  local copies, waits for them, and re-layouts: 7.38 us -> 0 us
  Pallas kernels: 91.4 us -> 85.8 us
  other arithmetic: 0 us -> 3.97 us
    unnamed x11 -> x0, local copies, waits for them, and re-layouts: 7.38 us -> none
    pallas_call x1, Pallas kernels: 91.4 us -> 85.8 us  [shards(): pl.pallas_call(kernel, out_shape=[tall] * 4 + [jax.ShapeDtypeStruct((CASE...]
    sub x0 -> x1, other arithmetic: none -> 3.97 us  [shards(): return (step + alpha * direction, rest - alpha * image)]
where the time goes in v2:
time: 90.5 us; the launch traced here: 90.4 us
  Pallas kernels  85.8 us (95%)
  other arithmetic  3.97 us (4%)
    pallas_call x1, Pallas kernels, shards(): pl.pallas_call(kernel, out_shape=[tall] * 4 + [jax.ShapeDtypeStruct((CASE...  85.8 us
    sub x1, other arithmetic, shards(): return (step + alpha * direction, rest - alpha * image)  3.97 us

profile of v2, /device:TPU:1, one launch (start us, length us, event | category | flops | bytes accessed | tf_op | source)
XLA Modules:
  0.0 90.4 jit_solution(1451911761050336025)
XLA Ops:
  0.6 85.8 %newton.1 = (f32[4,32,2048]{2,1,0:T(8,128)}, f32[4,32,2048]{2,1,0:T(8,128)}, f32[4,32,2048]{2,1,0:T(8,128)}, f32[4,32,2048]{2,1,0:T(8,128)}, f32[4,2048]{1,0:T(4,128)}) custom-call(f32[4,32,2048]{2,1,0:T(8,128)} %v_in.1, f32[4,32,2048]{2,1,0:T(8,128)} %photo_in.1, f32[32,2048]{1,0:T(8,128)} %shunt_in.1, f32[32,2048]{1,0:T(8,128)} %series_in.1, ...), custom_call_target="tpu_custom_call" | custom-call | tf_op jit(solution)/shard_map/newton/pallas_call | solution.py:671
  86.4 4.0 %multiply_subtract_fusion = (f32[4,32,2048]{2,1,0:T(8,128)}, f32[4,32,2048]{2,1,0:T(8,128)}) fusion(f32[4,32,2048]{2,1,0:T(8,128)} %get-tuple-element.10, f32[4,32,2048]{2,1,0:T(8,128)} %get-tuple-element.11, f32[4,2048]{1,0:T(4,128)} %get-tuple-element.8, f32[4,32,2048]{2,1,0:T(8,128)} %get-tuple-element.7, f32[4,32,2048]{2,1,0:T(8,128)} %get-tuple-element.9), kind=kLoop, calls=%fused_computation | loop fusion | flops 1048576 | bytes 6324224 | tf_op jit(solution)/shard_map/sub | solution.py:681

commit v3 on v2

--- a/solution.py
+++ b/solution.py
@@ -18,6 +18,7 @@
 FIELD = (BLOCKS + 2) * STEP
 NS = 16
 NC = 8
+CHIPS = NS // 2
 SOLVES = 3
 LEVELS = (0.25, 0.5, 1.0, 2.0)
 
@@ -38,14 +39,15 @@
     ef, rf, qf, df, xf, uf, wf, dgf, inf, pcf,
     sf, rlf, llf, dmf,
     cb, gm, e_low, m_high, groups, e_turn, ones_pair, ones_wide,
-    bu, bw, bq, sd, ss, su, er, el, lb,
+    bu, bw, bq, br, sd, ss, su, er, el, lb,
     pk, turned, su_s, sd_s, sl_s, sr_s, su_r, sd_r, sl_r, sr_r,
     hu_s, hd_s, hl_s, hr_s, hu_r, hd_r, hl_r, hr_r,
     s1, r1, s2, r2, s3, r3, s4, r4, fs, fr,
-    y_now, t_now, t_tile, state, per_case, local,
-    in_sem, setup_send, setup_recv, halo_send, halo_recv, send_sem, recv_sem, last_send, last_recv,
+    y_now, t_now, t_tile, state, per_case, local, local_w, sc_s, sc_r,
+    in_sem, setup_send, setup_recv, halo_send, halo_recv, send_sem, recv_sem, last_send, last_recv, sc_send, sc_recv,
 ):
     s = lax.axis_index("str")
+    chip = s // 2
     c = lax.axis_index("crs")
 
     def at_str(k):
@@ -71,6 +73,8 @@
     everyone = sorted(itertools.product(range(2), range(4), range(2), range(2), range(4)), key=far_first)[:-1]
     everyone = [(key, (str_at[key[:3]], crs_at[key[3:]])) for key in everyone]
     str_peers = [(who[0], c) for key, who in everyone if key[3:] == (0, 0)]
+    chip_peers = [(who[0], c) for key, who in everyone if key[2:] == (0, 0, 0)]
+    sibling = (str_at[(0, 0, 1)], c)
     crs_peers = [(s, who[1]) for key, who in everyone if key[:3] == (0, 0, 0)]
 
     barrier = pltpu.get_barrier_semaphore()
@@ -86,7 +90,7 @@
         pltpu.make_async_copy(shunt_in, shn, in_sem.at[5]),
         pltpu.make_async_copy(photo_in, pn, in_sem.at[6]),
     ]
-    quarter = pl.multiple_of((s // 4) * 128, 128)
+    quarter = pl.multiple_of((chip // 2) * 128, 128)
     for k in range(NC):
         loads.append(
             pltpu.make_async_copy(
@@ -186,6 +190,18 @@
     def spread(x, column, rows=ROWS):
         return jnp.broadcast_to(x[:, column : column + 1], (rows, 128))
 
+    def clear(i, _):
+        rows = pl.ds(pl.multiple_of(i * 80, 16), 80)
+        for f in (ef, wf, qf, df, xf):
+            f[rows, :] = jnp.zeros((80, 128), F32)
+        return 0
+
+    lax.fori_loop(0, CASES * FIELD // 80, clear, 0)
+    sf[...] = jnp.zeros_like(sf)
+    bw[...] = jnp.zeros_like(bw)
+    bq[...] = jnp.zeros_like(bq)
+    state[...] = jnp.zeros_like(state)
+    per_case[...] = jnp.zeros_like(per_case)
     for copy in loads[:5]:
         copy.wait()
     level = jnp.zeros((BLOCKS, ROWS), F32)
@@ -225,7 +241,7 @@
         group = spread(packed, j).astype(jnp.int32)
         groups[base : base + ROWS, :] = group
         low = group // 32
-        code = (low % 16) * 8 + low // 16
+        code = (low % 16) // 2 * 16 + low // 16 * 2 + low % 2
         lb[j * ROWS : j * ROWS + ROWS, 0:128] = (lane == code).astype(F32).astype(BF16)
         dmf[j * ROWS : j * ROWS + ROWS, :] = spread(packed, 32 + j)
     for k in range(4):
@@ -241,56 +257,13 @@
         ones_wide[0:128, case * 128 : case * 128 + 128] = wide
         ones_wide[128:256, case * 128 : case * 128 + 128] = wide
 
-    for copy in loads[7:]:
-        copy.wait()
-
-    def pick(i, _):
-        rows = pl.ds(pl.multiple_of(i * 32, 32), 32)
-        for side in range(2):
-            block = jnp.zeros((ROWS, 128), F32)
-            for k in range(4):
-                turn = lax.rem(32 * k + 128 - 32 * lax.rem(s, 4), 128)
-                block = jnp.where(case_of == k, pltpu.roll(staged[side * 4 + k, rows, :], turn, 1), block)
-            high, low = halves(block)
-            a_high[rows, side * 128 : side * 128 + 128] = high
-            a_low[rows, side * 128 : side * 128 + 128] = low
-        return 0
-
-    lax.fori_loop(0, 16, pick, 0)
-    for copy in loads[5:7]:
-        copy.wait()
-
-
-    for copy in setup_copies:
-        copy.wait()
-    edges_in(ef, sd_r, su_r, sl_r, sr_r)
-    sf[pl.ds(STEP - 1, BLOCKS, stride=STEP), :] = sd_r[72:88, :]
-    above8 = sd_r[64:72, :]
-    below8 = su_r[64:72, :]
-    for j in range(BLOCKS):
-        base = (j + 1) * STEP
-        groups[base - 1 : base, :] = spread(above8, j, 8)[7:8].astype(jnp.int32)
-        groups[base + ROWS : base + ROWS + 1, :] = spread(below8, j, 8)[0:1].astype(jnp.int32)
-    packed_left = jnp.broadcast_to(sl_r[1:2, :], (128, 128)).T[0:ROWS]
-    packed_right = jnp.broadcast_to(sr_r[1:2, :], (128, 128)).T[0:ROWS]
-    groups[0:ROWS, :] = packed_left.astype(jnp.int32)
-    groups[17 * STEP : 17 * STEP + ROWS, :] = packed_right.astype(jnp.int32)
-    level_left = jnp.broadcast_to(sl_r[2:3, :], (128, 128)).T[0:ROWS]
-    level_right = jnp.broadcast_to(sr_r[2:3, :], (128, 128)).T[0:ROWS]
-
-    open_left = jnp.where(c == 0, 0.0, 1.0).astype(F32)
-    open_right = jnp.where(c == NC - 1, 0.0, 1.0).astype(F32)
-    row_levels = (
-        [level_left] + [spread(packed, 16 + j) for j in range(BLOCKS)] + [level_right]
-    )
+    row_levels = [spread(packed, 16 + j) for j in range(BLOCKS)]
+    blank = jnp.zeros((ROWS, 128), F32)
+    row_levels = [blank] + row_levels + [blank]
     for j in range(BLOCKS):
         here = row_levels[j + 1]
         right = jnp.minimum(here, row_levels[j + 2])
         left = jnp.minimum(here, row_levels[j])
-        if j == BLOCKS - 1:
-            right = right * open_right
-        if j == 0:
-            left = left * open_left
         rlf[j * ROWS : j * ROWS + ROWS, :] = jnp.where(is_last, right, here)
         llf[j * ROWS : j * ROWS + ROWS, :] = jnp.where(is_first, left, here)
         er[j * ROWS : j * ROWS + ROWS, :] = right
@@ -319,6 +292,8 @@
         return 0
 
     lax.fori_loop(0, FIELD // 80, codes, 0)
+    for copy in loads[5:7]:
+        copy.wait()
 
     def start_rest(j, _):
         base = pl.multiple_of((j + 1) * STEP, 8)
@@ -344,7 +319,7 @@
             dgf[at, :] = slope
             rf[at, :] = rest
             rests.append(rest)
-        to_scatter(j, base, block_columns(j, base, rests, None))
+        block_columns(j, base, rests, br)
         return 0
 
     def start_scaled(j, sums):
@@ -375,18 +350,97 @@
     zero = jnp.zeros((8, 128), F32)
     lax.fori_loop(0, BLOCKS, start_rest, 0)
 
+    for copy in setup_copies:
+        copy.wait()
+    edges_in(ef, sd_r, su_r, sl_r, sr_r)
+    sf[pl.ds(STEP - 1, BLOCKS, stride=STEP), :] = sd_r[72:88, :]
+    open_left = jnp.where(c == 0, 0.0, 1.0).astype(F32)
+    open_right = jnp.where(c == NC - 1, 0.0, 1.0).astype(F32)
+    level_left = jnp.broadcast_to(sl_r[2:3, :], (128, 128)).T[0:ROWS]
+    level_right = jnp.broadcast_to(sr_r[2:3, :], (128, 128)).T[0:ROWS]
+    for block, slot, level_there, is_open, is_edge, link, edge in (
+        (0, 0, level_left, open_left, is_first, llf, el),
+        (BLOCKS - 1, BLOCKS + 1, level_right, open_right, is_last, rlf, er),
+    ):
+        rows = pl.ds(block * ROWS, ROWS)
+        here = row_levels[block + 1]
+        value = jnp.minimum(here, level_there) * is_open
+        link[rows, :] = jnp.where(is_edge, value, here)
+        edge[rows, :] = value
+        total = br[rows, :]
+        for case in range(CASES):
+            at = pl.ds(case * FIELD + (block + 1) * STEP, ROWS)
+            there = ef[pl.ds(case * FIELD + slot * STEP, ROWS), :]
+            more = jnp.where(is_edge, value * (there - ef[at, :]), 0.0)
+            rf[at, :] = rf[at, :] + more
+            total = total + jnp.where(case_of == case, jnp.sum(more, axis=1, keepdims=True), 0.0)
+        br[rows, :] = total
+    for first in (True, False):
+        edge_row = 0 if first else ROWS - 1
+        link = sf[pl.ds(STEP + (-1 if first else edge_row), BLOCKS, stride=STEP), :]
+        rows = pl.ds(edge_row, BLOCKS, stride=ROWS)
+        total = br[rows, :]
+        for case in range(CASES):
+            if first:
+                more = link * (ef[rows_of(case, -1), :] - ef[rows_of(case, 0), :])
+            else:
+                more = link * ef[rows_of(case, ROWS), :]
+            rf[rows_of(case, edge_row), :] = rf[rows_of(case, edge_row), :] + more
+            total = total + jnp.where(case_of[0:BLOCKS] == case, jnp.sum(more, axis=1, keepdims=True), 0.0)
+        br[rows, :] = total
+
+    def scatter_rest(j, _):
+        to_scatter(j, pl.multiple_of((j + 1) * STEP, 8), br[pl.ds(pl.multiple_of(j * ROWS, ROWS), ROWS), :])
+        return 0
+
+    lax.fori_loop(0, BLOCKS, scatter_rest, 0)
+
+    def prepare_rest():
+        above8 = sd_r[64:72, :]
+        below8 = su_r[64:72, :]
+        for j in range(BLOCKS):
+            base = (j + 1) * STEP
+            groups[base - 1 : base, :] = spread(above8, j, 8)[7:8].astype(jnp.int32)
+            groups[base + ROWS : base + ROWS + 1, :] = spread(below8, j, 8)[0:1].astype(jnp.int32)
+        for first, row_there in ((0, sl_r[1:2, :]), (17 * STEP, sr_r[1:2, :])):
+            groups[first : first + ROWS, :] = jnp.broadcast_to(row_there, (128, 128)).T[0:ROWS].astype(jnp.int32)
+        lax.fori_loop(0, FIELD // 80, codes, 0)
+        for copy in loads[7:]:
+            copy.wait()
+
+        def pick(i, _):
+            rows = pl.ds(pl.multiple_of(i * 32, 32), 32)
+            for block in range(4):
+                parts = []
+                for half in range(2):
+                    turn = lax.rem(64 * half + 128 - 64 * lax.rem(chip, 2), 128)
+                    parts.append(pltpu.roll(staged[block * 2 + half, rows, :], turn, 1))
+                high, low = halves(jnp.where(lane < 64, parts[0], parts[1]))
+                a_high[rows, block * 128 : block * 128 + 128] = high
+                a_low[rows, block * 128 : block * 128 + 128] = low
+            return 0
+
+        lax.fori_loop(0, 16, pick, 0)
+
 
     def send_restricted(k):
         out = dot(e_turn[...], lb[...])
-        s1[k] = (out[:, 0:128] + out[:, 128:256]).reshape(NS, 8, 128)
+        s1[k] = (out[:, 0:128] + out[:, 128:256]).reshape(CHIPS, 16, 128)
         for who in str_peers:
-            remote(s1.at[k, who[0]], r1.at[k, s], send_sem.at[k, 0], recv_sem.at[k, 0], who).start()
-        r1[k, s] = s1[k, s]
-
-    def send_chunk(k, scalars):
+            remote(s1.at[k, who[0] // 2], r1.at[k, s], send_sem.at[k, 0], recv_sem.at[k, 0], who).start()
+        r1[k, s] = s1[k, chip]
+
+    def swap_sums(k, tile):
+        sc_s[k] = tile
+        copy = remote(sc_s.at[k], sc_r.at[k], sc_send.at[k], sc_recv.at[k], sibling)
+        copy.start()
+        return copy
+
+    def send_chunk(k, swap):
+        swap.wait()
         arrived(r1.at[k, 0 : NS - 1], recv_sem.at[k, 0])
-        s2[k, 0:8, :] = jnp.sum(r1[k], axis=0)
-        s2[k, 8:16, :] = scalars
+        s2[k, 0:16, :] = jnp.sum(r1[k], axis=0)
+        s2[k, 16:24, :] = sc_s[k] + sc_r[k]
         for who in crs_peers:
             remote(s2.at[k], r2.at[k, c], send_sem.at[k, 1], recv_sem.at[k, 1], who).start()
         r2[k, c] = s2[k]
@@ -394,40 +448,43 @@
     def send_product(k):
         arrived(r2.at[k, 0 : NC - 1], recv_sem.at[k, 1])
         total = jnp.sum(r2[k], axis=0)
-        t = total[0:8]
+        t = total[0:16]
         t_tile[...] = t
-        placed = jnp.concatenate([jnp.broadcast_to(t[i : i + 1], (ROWS, 128)) * spot for i in range(NC)], axis=0)
+        placed = jnp.concatenate([jnp.broadcast_to(t[i : i + 1], (ROWS, 128)) * spot for i in range(16)], axis=0)
         high, low = halves(placed)
         both = dot(jnp.concatenate([high, low], axis=0), ones_pair[0:128, :]).astype(BF16)
-        right = jnp.concatenate([both[0:256], both[256:512]], axis=1)
+        right = jnp.concatenate([both[0:512], both[512:1024]], axis=1)
         out = dot(a_high[...], right)
-        out = out[:, 0:128] + out[:, 128:256] + dot(a_low[...], both[0:256])
+        out = out[:, 0:128] + out[:, 128:256] + dot(a_low[...], both[0:512])
         y = jnp.sum(out.reshape(16, ROWS, 128) * spot[None], axis=1)
         s3[k, 0:16, :] = y
-        own = t_tile[pl.ds(c, 1), :]
-        s3[k, 16:24, :] = jnp.where(sub8 == 0, jnp.broadcast_to(own, (8, 128)), total[8:16])
-        for who in str_peers:
-            remote(s3.at[k], r3.at[k, s], send_sem.at[k, 2], recv_sem.at[k, 2], who).start()
-        r3[k, s] = s3[k]
+        tile = total[16:24]
+        for i in range(2):
+            own = t_tile[pl.ds(2 * c + i, 1), :]
+            tile = jnp.where(sub8 == i, jnp.broadcast_to(own, (8, 128)), tile)
+        s3[k, 16:24, :] = tile
+        for who in chip_peers:
+            remote(s3.at[k], r3.at[k, chip], send_sem.at[k, 2], recv_sem.at[k, 2], who).start()
+        r3[k, chip] = s3[k]
 
     RZ, RR, ALPHA, BETA, RQ, QQ = range(6)
 
     def row(x, i):
         return jnp.broadcast_to(x[i : i + 1], (8, 128))
 
-    def send_correction(k):
-        arrived(r3.at[k, 0 : NS - 1], recv_sem.at[k, 2])
+    def send_correction(k, first=False):
+        arrived(r3.at[k, 0 : CHIPS - 1], recv_sem.at[k, 2])
         total = jnp.sum(r3[k], axis=0)
         y = total[0:16]
-        t = jnp.concatenate([r3[k, i, 16:17, :] for i in range(NS)], axis=0)
+        t = jnp.concatenate([r3[k, i, 16:18, :] for i in range(CHIPS)], axis=0)
         sums = total[16:24]
-        if k == 0:
-            state[RR] = row(sums, 1)
+        if first:
+            state[RR] = row(sums, 2)
         else:
-            alpha = state[RZ] / row(sums, 1)
+            alpha = state[RZ] / row(sums, 2)
             state[ALPHA] = alpha
-            state[QQ] = row(sums, 2)
-            state[RQ] = row(sums, 3)
+            state[QQ] = row(sums, 3)
+            state[RQ] = row(sums, 4)
             y = y_now[...] - alpha[0:1] * y
             t = t_now[...] - alpha[0:1] * t
         y_now[...] = y
@@ -442,7 +499,7 @@
         for case in range(CASES):
             per_case[slot, case] = jnp.broadcast_to(x[:, case * 32 : case * 32 + 1], (8, 128))
 
-    def receive_correction(k):
+    def receive_correction(k, first=False):
         arrived(r4.at[k, 0 : NC - 1], recv_sem.at[k, 3])
         correction = jnp.concatenate([r4[k, i, 0:16, :] for i in range(NC)], axis=0)
         high, low = halves(correction)
@@ -452,7 +509,7 @@
         gm[:, 128:256] = (picked[:, 128:256] * mask).astype(BF16)
         cb[...] = dot(gm[...], ones_pair[...])
         coarse = case_sums(jnp.sum(r4[k, :, 16:24, :], axis=0))
-        if k == 0:
+        if first:
             state[RZ] = state[RR] + coarse
         else:
             alpha = state[ALPHA]
@@ -464,20 +521,17 @@
             to_cases(0, alpha)
             to_cases(1, state[BETA])
 
-    def block_level(k):
+    def block_level(final=False):
         alpha = state[ALPHA][0:1]
         beta = state[BETA][0:1]
-        final = k == SOLVES - 1
 
         def body(j, energy):
             base = pl.multiple_of((j + 1) * STEP, 8)
             flat = pl.ds(pl.multiple_of(j * ROWS, ROWS), ROWS)
-            value = bu[flat, :]
-            if k:
-                value = value - alpha * bw[flat, :]
-                if not final:
-                    bu[flat, :] = value
-                value = value + beta * bq[flat, :]
+            value = bu[flat, :] - alpha * bw[flat, :]
+            if not final:
+                bu[flat, :] = value
+            value = value + beta * bq[flat, :]
             here = cb[pl.ds(base, ROWS), :]
             stencil = (
                 sd[flat, :] * here
@@ -501,10 +555,9 @@
         for case in range(CASES):
             pcf[case * FIELD : case * FIELD + FIELD, :] = wide[:, case * 128 : case * 128 + 128]
 
-    def next_direction(k):
+    def next_direction(final=False):
         widen_correction()
-        final = k == SOLVES - 1
-        kinds = {0: 3, SOLVES - 2: 5, SOLVES - 1: 0}[k]
+        kinds = 0 if final else 5
 
         def body(j, sums):
             base = pl.multiple_of((j + 1) * STEP, 8)
@@ -516,32 +569,24 @@
                 here, image = jacobian(pcf, case, base, link)
                 rest = rf[at, :]
                 inverse = inf[at, :]
-                smooth = uf[at, :]
-                if k:
-                    alpha = per_case[0, case][0:1]
-                    beta = per_case[1, case][0:1]
-                    last_image = qf[at, :]
-                    last_direction = df[at, :]
-                    smooth = smooth - alpha * wf[at, :]
-                    image = image + beta * last_image
-                    rest = rest - alpha * last_image
-                    step = alpha * last_direction
-                    if k > 1:
-                        step = step + xf[at, :]
-                image = image + smooth
-                direction = rest * inverse + here
-                if k:
-                    direction = direction + beta * last_direction
+                alpha = per_case[0, case][0:1]
+                beta = per_case[1, case][0:1]
+                last_image = qf[at, :]
+                last_direction = df[at, :]
+                smooth = uf[at, :] - alpha * wf[at, :]
+                image = image + beta * last_image + smooth
+                rest = rest - alpha * last_image
+                step = xf[at, :] + alpha * last_direction
+                direction = rest * inverse + here + beta * last_direction
                 if final:
                     xf_out[case, :, cols] = step
                     rf_out[case, :, cols] = rest
                     df_out[case, :, cols] = direction
                     qf_out[case, :, cols] = image
                     continue
-                if k:
-                    uf[at, :] = smooth
-                    rf[at, :] = rest
-                    xf[at, :] = step
+                uf[at, :] = smooth
+                rf[at, :] = rest
+                xf[at, :] = step
                 qf[at, :] = image
                 df[at, :] = direction
                 scaled = image * inverse
@@ -554,7 +599,7 @@
         tile = zero
         for kind in range(kinds):
             one = by_case([sums[kinds * case + kind] for case in range(CASES)])
-            tile = jnp.where(sub8 == kind + 1, one, tile)
+            tile = jnp.where(sub8 == kind + 2, one, tile)
         return tile
 
     def start_halo(k):
@@ -575,44 +620,48 @@
                 here, image = jacobian(ef, case, base, link)
                 target[pl.ds(case * FIELD + base, ROWS), :] = image
                 values.append(image)
-                if k == SOLVES - 1:
-                    out.append(sums[case] + fold(here * image))
+                out.append(sums[case] + fold(here * image))
             block_columns(j, base, values, sums_to)
             return tuple(out)
 
-        return lax.fori_loop(0, BLOCKS, body, (zero,) * (CASES if k == SOLVES - 1 else 0))
+        return lax.fori_loop(0, BLOCKS, body, (zero,) * CASES)
 
 
     send_restricted(0)
     start_sums = lax.fori_loop(0, BLOCKS, start_scaled, (zero,) * CASES)
-    tile = jnp.where(sub8 == 1, by_case(start_sums), zero)
+    swap = swap_sums(0, jnp.where(sub8 == 2, by_case(start_sums), zero))
     copies = start_halo(0)
-    send_chunk(0, tile)
+    send_chunk(0, swap)
+    prepare_rest()
+    send_product(0)
     apply_scaled(0, copies, uf, bu)
-    send_product(0)
-    send_correction(0)
-    receive_correction(0)
-    for k in range(1, SOLVES):
-        block_level(k - 1)
+    send_correction(0, first=True)
+    receive_correction(0, first=True)
+
+    def solve(k, _):
+        block_level()
         send_restricted(k)
-        tile = next_direction(k - 1)
-        if k == SOLVES - 1:
-            local[...] = tile
+        tile = next_direction()
+        local[...] = tile
+        swap = swap_sums(k, tile)
         copies = start_halo(k)
-        send_chunk(k, tile)
+        send_chunk(k, swap)
         send_product(k)
-        scaled_sums = apply_scaled(k, copies, wf, bw)
+        local_w[...] = by_case(apply_scaled(k, copies, wf, bw))
         send_correction(k)
         receive_correction(k)
+        return 0
+
+    lax.fori_loop(1, SOLVES, solve, 0)
 
 
     alpha = state[ALPHA]
     beta = state[BETA]
-    energy = jnp.sum(block_level(SOLVES - 1), axis=0, keepdims=True)
-    dq, qq, rq, eu, qu = (row(local[...], i) for i in range(1, 6))
+    energy = jnp.sum(block_level(final=True), axis=0, keepdims=True)
+    dq, qq, rq, eu, qu = (row(local[...], i) for i in range(2, 7))
     energy = (
         energy
-        + (eu - 2.0 * alpha * qu + alpha * alpha * by_case(scaled_sums))
+        + (eu - 2.0 * alpha * qu + alpha * alpha * local_w[...])
         + 2.0 * beta * (rq - alpha * qq)
         + beta * beta * dq
     )
@@ -621,7 +670,7 @@
     for _, who in everyone:
         remote(fs, fr.at[here], last_send.at[0], last_recv.at[0], who).start()
     fr[here] = fs[...]
-    next_direction(SOLVES - 1)
+    next_direction(final=True)
     arrived(fr.at[0 : NS * NC - 1], last_recv.at[0])
     alpha = state[RZ] / jnp.broadcast_to(jnp.sum(fr[...], axis=0), (8, 128))
     for case in range(CASES):
@@ -631,7 +680,7 @@
     for k in range(SOLVES):
         arrived(r1.at[k, 0 : NS - 1], send_sem.at[k, 0])
         arrived(r2.at[k, 0 : NC - 1], send_sem.at[k, 1])
-        arrived(r3.at[k, 0 : NS - 1], send_sem.at[k, 2])
+        arrived(r3.at[k, 0 : CHIPS - 1], send_sem.at[k, 2])
         arrived(r4.at[k, 0 : NC - 1], send_sem.at[k, 3])
     arrived(fr.at[0 : NS * NC - 1], last_send.at[0])
 
@@ -647,25 +696,26 @@
     scratch = [
         vmem((CASES, ROWS, 2048)), vmem((CASES, ROWS, 2048)), vmem((ROWS, 2048)), vmem((ROWS, 2048)),
         vmem((BLOCKS, ROWS), jnp.int32), vmem((BLOCKS, ROWS), jnp.int32), vmem((BLOCKS, ROWS), jnp.int32),
-        vmem((NC, 512, 128)), vmem((512, 256), BF16), vmem((512, 256), BF16),
+        vmem((NC, 512, 128)), vmem((512, 512), BF16), vmem((512, 512), BF16),
         *[vmem(field) for _ in range(10)],
         vmem((FIELD, 128)), vmem(flat), vmem(flat), vmem(flat),
         vmem((FIELD, 128)), vmem((FIELD, 256), BF16), vmem((FIELD, 128), BF16), vmem((FIELD, 128)),
         vmem((FIELD, 128), jnp.int32), vmem((128, 512), BF16), vmem((256, 128), BF16), vmem((256, 512), BF16),
-        *[vmem(flat) for _ in range(8)], vmem((512, 256), BF16),
+        *[vmem(flat) for _ in range(9)], vmem((512, 256), BF16),
         vmem((ROWS, 128)), vmem((128, 128)),
         vmem((72, 128)), vmem((88, 128)), vmem((8, 128)), vmem((8, 128)),
         vmem((72, 128)), vmem((88, 128)), vmem((8, 128)), vmem((8, 128)),
         vmem((SOLVES, 64, 128)), vmem((SOLVES, 64, 128)), vmem((SOLVES, 8, 128)), vmem((SOLVES, 8, 128)),
         vmem((SOLVES, 64, 128)), vmem((SOLVES, 64, 128)), vmem((SOLVES, 8, 128)), vmem((SOLVES, 8, 128)),
-        vmem((SOLVES, NS, 8, 128)), vmem((SOLVES, NS, 8, 128)),
-        vmem((SOLVES, 16, 128)), vmem((SOLVES, NC, 16, 128)),
-        vmem((SOLVES, 24, 128)), vmem((SOLVES, NS, 24, 128)),
+        vmem((SOLVES, CHIPS, 16, 128)), vmem((SOLVES, NS, 16, 128)),
+        vmem((SOLVES, 24, 128)), vmem((SOLVES, NC, 24, 128)),
+        vmem((SOLVES, 24, 128)), vmem((SOLVES, CHIPS, 24, 128)),
         vmem((SOLVES, 24, 128)), vmem((SOLVES, NC, 24, 128)),
         vmem((1, 128)), vmem((NS * NC, 1, 128)),
-        vmem((16, 128)), vmem((16, 128)), vmem((8, 128)), vmem((6, 8, 128)), vmem((2, CASES, 8, 128)), vmem((8, 128)),
+        vmem((16, 128)), vmem((16, 128)), vmem((16, 128)), vmem((6, 8, 128)), vmem((2, CASES, 8, 128)), vmem((8, 128)), vmem((8, 128)),
+        vmem((SOLVES, 8, 128)), vmem((SOLVES, 8, 128)),
         dma((15,)), dma((4,)), dma((4,)), dma((SOLVES, 4)), dma((SOLVES, 4)),
-        dma((SOLVES, 4)), dma((SOLVES, 4)), dma((1,)), dma((1,)),
+        dma((SOLVES, 4)), dma((SOLVES, 4)), dma((1,)), dma((1,)), dma((SOLVES,)), dma((SOLVES,)),
     ]
     tall = jax.ShapeDtypeStruct((CASES, ROWS, 2048), F32)
     step, direction, rest, image, alpha = pl.pallas_call(

time: 90.5 us -> 87 us (0.961)
  Pallas kernels: 85.8 us -> 82.3 us
    pallas_call x1, Pallas kernels: 85.8 us -> 82.3 us  [shards(): pl.pallas_call(kernel, out_shape=[tall] * 4 + [jax.ShapeDtypeStruct((CASE...]
where the time goes in v3:
time: 87 us; the launch traced here: 86.9 us
  Pallas kernels  82.3 us (95%)
  other arithmetic  3.97 us (5%)
    pallas_call x1, Pallas kernels, shards(): pl.pallas_call(kernel, out_shape=[tall] * 4 + [jax.ShapeDtypeStruct((CASE...  82.3 us
    sub x1, other arithmetic, shards(): return (step + alpha * direction, rest - alpha * image)  3.97 us

profile of v3, /device:TPU:1, one launch (start us, length us, event | category | flops | bytes accessed | tf_op | source)
XLA Modules:
  0.0 86.9 jit_solution(15268624546117351362)
XLA Ops:
  0.6 82.3 %newton.1 = (f32[4,32,2048]{2,1,0:T(8,128)}, f32[4,32,2048]{2,1,0:T(8,128)}, f32[4,32,2048]{2,1,0:T(8,128)}, f32[4,32,2048]{2,1,0:T(8,128)}, f32[4,2048]{1,0:T(4,128)}) custom-call(f32[4,32,2048]{2,1,0:T(8,128)} %v_in.1, f32[4,32,2048]{2,1,0:T(8,128)} %photo_in.1, f32[32,2048]{1,0:T(8,128)} %shunt_in.1, f32[32,2048]{1,0:T(8,128)} %series_in.1, ...), custom_call_target="tpu_custom_call" | custom-call | tf_op jit(solution)/shard_map/newton/pallas_call | solution.py:721
  82.9 4.0 %multiply_subtract_fusion = (f32[4,32,2048]{2,1,0:T(8,128)}, f32[4,32,2048]{2,1,0:T(8,128)}) fusion(f32[4,32,2048]{2,1,0:T(8,128)} %get-tuple-element.10, f32[4,32,2048]{2,1,0:T(8,128)} %get-tuple-element.11, f32[4,2048]{1,0:T(4,128)} %get-tuple-element.8, f32[4,32,2048]{2,1,0:T(8,128)} %get-tuple-element.7, f32[4,32,2048]{2,1,0:T(8,128)} %get-tuple-element.9), kind=kLoop, calls=%fused_computation | loop fusion | flops 1048576 | bytes 6324224 | tf_op jit(solution)/shard_map/sub | solution.py:731

commit v4 on v3

--- a/solution.py
+++ b/solution.py
@@ -18,7 +18,6 @@
 FIELD = (BLOCKS + 2) * STEP
 NS = 16
 NC = 8
-CHIPS = NS // 2
 SOLVES = 3
 LEVELS = (0.25, 0.5, 1.0, 2.0)
 
@@ -35,7 +34,7 @@
 def kernel(
     v_in, photo_in, shunt_in, series_in, pattern_in, mask_in, group_in, inverse_in,
     xf_out, df_out, rf_out, qf_out, alpha_out,
-    vn, pn, shn, sn, patn, maskn, groupn, staged, a_high, a_low,
+    xn, dn, vn, pn, shn, sn, patn, maskn, groupn, staged, a_high, a_low,
     ef, rf, qf, df, xf, uf, wf, dgf, inf, pcf,
     sf, rlf, llf, dmf,
     cb, gm, e_low, m_high, groups, e_turn, ones_pair, ones_wide,
@@ -43,11 +42,10 @@
     pk, turned, su_s, sd_s, sl_s, sr_s, su_r, sd_r, sl_r, sr_r,
     hu_s, hd_s, hl_s, hr_s, hu_r, hd_r, hl_r, hr_r,
     s1, r1, s2, r2, s3, r3, s4, r4, fs, fr,
-    y_now, t_now, t_tile, state, per_case, local, local_w, sc_s, sc_r,
-    in_sem, setup_send, setup_recv, halo_send, halo_recv, send_sem, recv_sem, last_send, last_recv, sc_send, sc_recv,
+    y_now, t_now, t_tile, state, per_case, local, local_w,
+    in_sem, out_sem, setup_send, setup_recv, halo_send, halo_recv, send_sem, recv_sem, last_send, last_recv,
 ):
     s = lax.axis_index("str")
-    chip = s // 2
     c = lax.axis_index("crs")
 
     def at_str(k):
@@ -73,8 +71,6 @@
     everyone = sorted(itertools.product(range(2), range(4), range(2), range(2), range(4)), key=far_first)[:-1]
     everyone = [(key, (str_at[key[:3]], crs_at[key[3:]])) for key in everyone]
     str_peers = [(who[0], c) for key, who in everyone if key[3:] == (0, 0)]
-    chip_peers = [(who[0], c) for key, who in everyone if key[2:] == (0, 0, 0)]
-    sibling = (str_at[(0, 0, 1)], c)
     crs_peers = [(s, who[1]) for key, who in everyone if key[:3] == (0, 0, 0)]
 
     barrier = pltpu.get_barrier_semaphore()
@@ -90,7 +86,7 @@
         pltpu.make_async_copy(shunt_in, shn, in_sem.at[5]),
         pltpu.make_async_copy(photo_in, pn, in_sem.at[6]),
     ]
-    quarter = pl.multiple_of((chip // 2) * 128, 128)
+    quarter = pl.multiple_of((s // 4) * 128, 128)
     for k in range(NC):
         loads.append(
             pltpu.make_async_copy(
@@ -241,7 +237,7 @@
         group = spread(packed, j).astype(jnp.int32)
         groups[base : base + ROWS, :] = group
         low = group // 32
-        code = (low % 16) // 2 * 16 + low // 16 * 2 + low % 2
+        code = (low % 16) * 8 + low // 16
         lb[j * ROWS : j * ROWS + ROWS, 0:128] = (lane == code).astype(F32).astype(BF16)
         dmf[j * ROWS : j * ROWS + ROWS, :] = spread(packed, 32 + j)
     for k in range(4):
@@ -410,14 +406,14 @@
 
         def pick(i, _):
             rows = pl.ds(pl.multiple_of(i * 32, 32), 32)
-            for block in range(4):
-                parts = []
-                for half in range(2):
-                    turn = lax.rem(64 * half + 128 - 64 * lax.rem(chip, 2), 128)
-                    parts.append(pltpu.roll(staged[block * 2 + half, rows, :], turn, 1))
-                high, low = halves(jnp.where(lane < 64, parts[0], parts[1]))
-                a_high[rows, block * 128 : block * 128 + 128] = high
-                a_low[rows, block * 128 : block * 128 + 128] = low
+            for side in range(2):
+                block = jnp.zeros((ROWS, 128), F32)
+                for k in range(4):
+                    turn = lax.rem(32 * k + 128 - 32 * lax.rem(s, 4), 128)
+                    block = jnp.where(case_of == k, pltpu.roll(staged[side * 4 + k, rows, :], turn, 1), block)
+                high, low = halves(block)
+                a_high[rows, side * 128 : side * 128 + 128] = high
+                a_low[rows, side * 128 : side * 128 + 128] = low
             return 0
 
         lax.fori_loop(0, 16, pick, 0)
@@ -425,22 +421,15 @@
 
     def send_restricted(k):
         out = dot(e_turn[...], lb[...])
-        s1[k] = (out[:, 0:128] + out[:, 128:256]).reshape(CHIPS, 16, 128)
+        s1[k] = (out[:, 0:128] + out[:, 128:256]).reshape(NS, 8, 128)
         for who in str_peers:
-            remote(s1.at[k, who[0] // 2], r1.at[k, s], send_sem.at[k, 0], recv_sem.at[k, 0], who).start()
-        r1[k, s] = s1[k, chip]
-
-    def swap_sums(k, tile):
-        sc_s[k] = tile
-        copy = remote(sc_s.at[k], sc_r.at[k], sc_send.at[k], sc_recv.at[k], sibling)
-        copy.start()
-        return copy
-
-    def send_chunk(k, swap):
-        swap.wait()
+            remote(s1.at[k, who[0]], r1.at[k, s], send_sem.at[k, 0], recv_sem.at[k, 0], who).start()
+        r1[k, s] = s1[k, s]
+
+    def send_chunk(k, tile):
         arrived(r1.at[k, 0 : NS - 1], recv_sem.at[k, 0])
-        s2[k, 0:16, :] = jnp.sum(r1[k], axis=0)
-        s2[k, 16:24, :] = sc_s[k] + sc_r[k]
+        s2[k, 0:8, :] = jnp.sum(r1[k], axis=0)
+        s2[k, 8:12, :] = tile[0:4]
         for who in crs_peers:
             remote(s2.at[k], r2.at[k, c], send_sem.at[k, 1], recv_sem.at[k, 1], who).start()
         r2[k, c] = s2[k]
@@ -448,24 +437,21 @@
     def send_product(k):
         arrived(r2.at[k, 0 : NC - 1], recv_sem.at[k, 1])
         total = jnp.sum(r2[k], axis=0)
-        t = total[0:16]
+        t = total[0:8]
         t_tile[...] = t
-        placed = jnp.concatenate([jnp.broadcast_to(t[i : i + 1], (ROWS, 128)) * spot for i in range(16)], axis=0)
+        placed = jnp.concatenate([jnp.broadcast_to(t[i : i + 1], (ROWS, 128)) * spot for i in range(NC)], axis=0)
         high, low = halves(placed)
         both = dot(jnp.concatenate([high, low], axis=0), ones_pair[0:128, :]).astype(BF16)
-        right = jnp.concatenate([both[0:512], both[512:1024]], axis=1)
+        right = jnp.concatenate([both[0:256], both[256:512]], axis=1)
         out = dot(a_high[...], right)
-        out = out[:, 0:128] + out[:, 128:256] + dot(a_low[...], both[0:512])
+        out = out[:, 0:128] + out[:, 128:256] + dot(a_low[...], both[0:256])
         y = jnp.sum(out.reshape(16, ROWS, 128) * spot[None], axis=1)
         s3[k, 0:16, :] = y
-        tile = total[16:24]
-        for i in range(2):
-            own = t_tile[pl.ds(2 * c + i, 1), :]
-            tile = jnp.where(sub8 == i, jnp.broadcast_to(own, (8, 128)), tile)
-        s3[k, 16:24, :] = tile
-        for who in chip_peers:
-            remote(s3.at[k], r3.at[k, chip], send_sem.at[k, 2], recv_sem.at[k, 2], who).start()
-        r3[k, chip] = s3[k]
+        own = t_tile[pl.ds(c, 1), :]
+        s3[k, 16:20, :] = jnp.where(sub8[0:4] == 0, jnp.broadcast_to(own, (4, 128)), total[8:12])
+        for who in str_peers:
+            remote(s3.at[k], r3.at[k, s], send_sem.at[k, 2], recv_sem.at[k, 2], who).start()
+        r3[k, s] = s3[k]
 
     RZ, RR, ALPHA, BETA, RQ, QQ = range(6)
 
@@ -473,24 +459,24 @@
         return jnp.broadcast_to(x[i : i + 1], (8, 128))
 
     def send_correction(k, first=False):
-        arrived(r3.at[k, 0 : CHIPS - 1], recv_sem.at[k, 2])
+        arrived(r3.at[k, 0 : NS - 1], recv_sem.at[k, 2])
         total = jnp.sum(r3[k], axis=0)
         y = total[0:16]
-        t = jnp.concatenate([r3[k, i, 16:18, :] for i in range(CHIPS)], axis=0)
-        sums = total[16:24]
+        t = jnp.concatenate([r3[k, i, 16:17, :] for i in range(NS)], axis=0)
+        sums = total[16:20]
         if first:
-            state[RR] = row(sums, 2)
+            state[RR] = row(sums, 1)
         else:
-            alpha = state[RZ] / row(sums, 2)
+            alpha = state[RZ] / row(sums, 1)
             state[ALPHA] = alpha
-            state[QQ] = row(sums, 3)
-            state[RQ] = row(sums, 4)
+            state[QQ] = row(sums, 2)
+            state[RQ] = row(sums, 3)
             y = y_now[...] - alpha[0:1] * y
             t = t_now[...] - alpha[0:1] * t
         y_now[...] = y
         t_now[...] = t
         s4[k, 0:16, :] = y
-        s4[k, 16:24, :] = jnp.broadcast_to(jnp.sum(y * t, axis=0, keepdims=True), (8, 128))
+        s4[k, 16:17, :] = jnp.sum(y * t, axis=0, keepdims=True)
         for who in crs_peers:
             remote(s4.at[k], r4.at[k, c], send_sem.at[k, 3], recv_sem.at[k, 3], who).start()
         r4[k, c] = s4[k]
@@ -508,7 +494,7 @@
         gm[:, 0:128] = (picked[:, 0:128] * mask).astype(BF16)
         gm[:, 128:256] = (picked[:, 128:256] * mask).astype(BF16)
         cb[...] = dot(gm[...], ones_pair[...])
-        coarse = case_sums(jnp.sum(r4[k, :, 16:24, :], axis=0))
+        coarse = case_sums(jnp.broadcast_to(jnp.sum(r4[k, :, 16:17, :], axis=0), (8, 128)))
         if first:
             state[RZ] = state[RR] + coarse
         else:
@@ -579,10 +565,10 @@
                 step = xf[at, :] + alpha * last_direction
                 direction = rest * inverse + here + beta * last_direction
                 if final:
-                    xf_out[case, :, cols] = step
-                    rf_out[case, :, cols] = rest
-                    df_out[case, :, cols] = direction
-                    qf_out[case, :, cols] = image
+                    xn[case, :, cols] = step
+                    vn[case, :, cols] = rest
+                    dn[case, :, cols] = direction
+                    pn[case, :, cols] = image
                     continue
                 uf[at, :] = smooth
                 rf[at, :] = rest
@@ -599,7 +585,7 @@
         tile = zero
         for kind in range(kinds):
             one = by_case([sums[kinds * case + kind] for case in range(CASES)])
-            tile = jnp.where(sub8 == kind + 2, one, tile)
+            tile = jnp.where(sub8 == kind + 1, one, tile)
         return tile
 
     def start_halo(k):
@@ -629,9 +615,9 @@
 
     send_restricted(0)
     start_sums = lax.fori_loop(0, BLOCKS, start_scaled, (zero,) * CASES)
-    swap = swap_sums(0, jnp.where(sub8 == 2, by_case(start_sums), zero))
+    tile = jnp.where(sub8 == 1, by_case(start_sums), zero)
     copies = start_halo(0)
-    send_chunk(0, swap)
+    send_chunk(0, tile)
     prepare_rest()
     send_product(0)
     apply_scaled(0, copies, uf, bu)
@@ -643,9 +629,8 @@
         send_restricted(k)
         tile = next_direction()
         local[...] = tile
-        swap = swap_sums(k, tile)
         copies = start_halo(k)
-        send_chunk(k, swap)
+        send_chunk(k, tile)
         send_product(k)
         local_w[...] = by_case(apply_scaled(k, copies, wf, bw))
         send_correction(k)
@@ -658,7 +643,7 @@
     alpha = state[ALPHA]
     beta = state[BETA]
     energy = jnp.sum(block_level(final=True), axis=0, keepdims=True)
-    dq, qq, rq, eu, qu = (row(local[...], i) for i in range(2, 7))
+    dq, qq, rq, eu, qu = (row(local[...], i) for i in range(1, 6))
     energy = (
         energy
         + (eu - 2.0 * alpha * qu + alpha * alpha * local_w[...])
@@ -671,16 +656,25 @@
         remote(fs, fr.at[here], last_send.at[0], last_recv.at[0], who).start()
     fr[here] = fs[...]
     next_direction(final=True)
+    stores = [
+        pltpu.make_async_copy(src, dst, out_sem.at[i])
+        for i, (src, dst) in enumerate(((xn, xf_out), (dn, df_out), (vn, rf_out), (pn, qf_out)))
+    ]
+    for copy in stores:
+        copy.start()
     arrived(fr.at[0 : NS * NC - 1], last_recv.at[0])
     alpha = state[RZ] / jnp.broadcast_to(jnp.sum(fr[...], axis=0), (8, 128))
     for case in range(CASES):
         alpha_out[case : case + 1, :] = jnp.broadcast_to(alpha[0:1, case * 32 : case * 32 + 1], (1, 2048))
 
 
+    for copy in stores:
+        copy.wait()
+
     for k in range(SOLVES):
         arrived(r1.at[k, 0 : NS - 1], send_sem.at[k, 0])
         arrived(r2.at[k, 0 : NC - 1], send_sem.at[k, 1])
-        arrived(r3.at[k, 0 : CHIPS - 1], send_sem.at[k, 2])
+        arrived(r3.at[k, 0 : NS - 1], send_sem.at[k, 2])
         arrived(r4.at[k, 0 : NC - 1], send_sem.at[k, 3])
     arrived(fr.at[0 : NS * NC - 1], last_send.at[0])
 
@@ -694,9 +688,9 @@
 
     dma = pltpu.SemaphoreType.DMA
     scratch = [
-        vmem((CASES, ROWS, 2048)), vmem((CASES, ROWS, 2048)), vmem((ROWS, 2048)), vmem((ROWS, 2048)),
+        *[vmem((CASES, ROWS, 2048)) for _ in range(4)], vmem((ROWS, 2048)), vmem((ROWS, 2048)),
         vmem((BLOCKS, ROWS), jnp.int32), vmem((BLOCKS, ROWS), jnp.int32), vmem((BLOCKS, ROWS), jnp.int32),
-        vmem((NC, 512, 128)), vmem((512, 512), BF16), vmem((512, 512), BF16),
+        vmem((NC, 512, 128)), vmem((512, 256), BF16), vmem((512, 256), BF16),
         *[vmem(field) for _ in range(10)],
         vmem((FIELD, 128)), vmem(flat), vmem(flat), vmem(flat),
         vmem((FIELD, 128)), vmem((FIELD, 256), BF16), vmem((FIELD, 128), BF16), vmem((FIELD, 128)),
@@ -707,22 +701,21 @@
         vmem((72, 128)), vmem((88, 128)), vmem((8, 128)), vmem((8, 128)),
         vmem((SOLVES, 64, 128)), vmem((SOLVES, 64, 128)), vmem((SOLVES, 8, 128)), vmem((SOLVES, 8, 128)),
         vmem((SOLVES, 64, 128)), vmem((SOLVES, 64, 128)), vmem((SOLVES, 8, 128)), vmem((SOLVES, 8, 128)),
-        vmem((SOLVES, CHIPS, 16, 128)), vmem((SOLVES, NS, 16, 128)),
-        vmem((SOLVES, 24, 128)), vmem((SOLVES, NC, 24, 128)),
-        vmem((SOLVES, 24, 128)), vmem((SOLVES, CHIPS, 24, 128)),
-        vmem((SOLVES, 24, 128)), vmem((SOLVES, NC, 24, 128)),
+        vmem((SOLVES, NS, 8, 128)), vmem((SOLVES, NS, 8, 128)),
+        vmem((SOLVES, 12, 128)), vmem((SOLVES, NC, 12, 128)),
+        vmem((SOLVES, 20, 128)), vmem((SOLVES, NS, 20, 128)),
+        vmem((SOLVES, 17, 128)), vmem((SOLVES, NC, 17, 128)),
         vmem((1, 128)), vmem((NS * NC, 1, 128)),
-        vmem((16, 128)), vmem((16, 128)), vmem((16, 128)), vmem((6, 8, 128)), vmem((2, CASES, 8, 128)), vmem((8, 128)), vmem((8, 128)),
-        vmem((SOLVES, 8, 128)), vmem((SOLVES, 8, 128)),
-        dma((15,)), dma((4,)), dma((4,)), dma((SOLVES, 4)), dma((SOLVES, 4)),
-        dma((SOLVES, 4)), dma((SOLVES, 4)), dma((1,)), dma((1,)), dma((SOLVES,)), dma((SOLVES,)),
+        vmem((16, 128)), vmem((16, 128)), vmem((8, 128)), vmem((6, 8, 128)), vmem((2, CASES, 8, 128)), vmem((8, 128)), vmem((8, 128)),
+        dma((15,)), dma((4,)), dma((4,)), dma((4,)), dma((SOLVES, 4)), dma((SOLVES, 4)),
+        dma((SOLVES, 4)), dma((SOLVES, 4)), dma((1,)), dma((1,)),
     ]
     tall = jax.ShapeDtypeStruct((CASES, ROWS, 2048), F32)
     step, direction, rest, image, alpha = pl.pallas_call(
         kernel,
         out_shape=[tall] * 4 + [jax.ShapeDtypeStruct((CASES, 2048), F32)],
         in_specs=[pl.BlockSpec(memory_space=pltpu.HBM)] * 8,
-        out_specs=[pl.BlockSpec(memory_space=pltpu.VMEM)] * 5,
+        out_specs=[pl.BlockSpec(memory_space=pltpu.HBM)] * 4 + [pl.BlockSpec(memory_space=pltpu.VMEM)],
         scratch_shapes=scratch,
         compiler_params=pltpu.CompilerParams(collective_id=0, has_side_effects=True, vmem_limit_bytes=54 * 2**20),
         name="newton",

time: 87 us -> 84.4 us (0.970)
  Pallas kernels: 82.3 us -> 79.7 us
    pallas_call x1, Pallas kernels: 82.3 us -> 79.7 us  [shards(): pl.pallas_call(kernel, out_shape=[tall] * 4 + [jax.ShapeDtypeStruct((CASE...]
where the time goes in v4:
time: 84.4 us; the launch traced here: 84.3 us
  Pallas kernels  79.7 us (94%)
  other arithmetic  3.97 us (5%)
    pallas_call x1, Pallas kernels, shards(): pl.pallas_call(kernel, out_shape=[tall] * 4 + [jax.ShapeDtypeStruct((CASE...  79.7 us
    sub x1, other arithmetic, shards(): return (step + alpha * direction, rest - alpha * image)  3.97 us

profile of v4, /device:TPU:1, one launch (start us, length us, event | category | flops | bytes accessed | tf_op | source)
XLA Modules:
  0.0 84.3 jit_solution(6554532246009902414)
XLA Ops:
  0.6 79.7 %newton.1 = (f32[4,32,2048]{2,1,0:T(8,128)}, f32[4,32,2048]{2,1,0:T(8,128)}, f32[4,32,2048]{2,1,0:T(8,128)}, f32[4,32,2048]{2,1,0:T(8,128)}, f32[4,2048]{1,0:T(4,128)}) custom-call(f32[4,32,2048]{2,1,0:T(8,128)} %v_in.1, f32[4,32,2048]{2,1,0:T(8,128)} %photo_in.1, f32[32,2048]{1,0:T(8,128)} %shunt_in.1, f32[32,2048]{1,0:T(8,128)} %series_in.1, ...), custom_call_target="tpu_custom_call" | custom-call | tf_op jit(solution)/shard_map/newton/pallas_call | solution.py:714
  80.3 4.0 %multiply_subtract_fusion = (f32[4,32,2048]{2,1,0:T(8,128)}, f32[4,32,2048]{2,1,0:T(8,128)}) fusion(f32[4,32,2048]{2,1,0:T(8,128)} %get-tuple-element.10, f32[4,32,2048]{2,1,0:T(8,128)} %get-tuple-element.11, f32[4,2048]{1,0:T(4,128)} %get-tuple-element.8, f32[4,32,2048]{2,1,0:T(8,128)} %get-tuple-element.7, f32[4,32,2048]{2,1,0:T(8,128)} %get-tuple-element.9), kind=kLoop, calls=%fused_computation | loop fusion | flops 1048576 | bytes 6324224 | tf_op jit(solution)/shard_map/sub | solution.py:724

commit v5 on v4

--- a/solution.py
+++ b/solution.py
@@ -389,7 +389,7 @@
         to_scatter(j, pl.multiple_of((j + 1) * STEP, 8), br[pl.ds(pl.multiple_of(j * ROWS, ROWS), ROWS), :])
         return 0
 
-    lax.fori_loop(0, BLOCKS, scatter_rest, 0)
+    lax.fori_loop(0, BLOCKS, scatter_rest, 0, unroll=4)
 
     def prepare_rest():
         above8 = sd_r[64:72, :]
@@ -480,6 +480,8 @@
         for who in crs_peers:
             remote(s4.at[k], r4.at[k, c], send_sem.at[k, 3], recv_sem.at[k, 3], who).start()
         r4[k, c] = s4[k]
+        if not first:
+            bu[...] = bu[...] - alpha[0:1] * bw[...]
 
     def to_cases(slot, x):
         for case in range(CASES):
@@ -504,20 +506,14 @@
             state[RR] = smooth
             state[BETA] = fresh / state[RZ]
             state[RZ] = fresh
-            to_cases(0, alpha)
-            to_cases(1, state[BETA])
 
     def block_level(final=False):
-        alpha = state[ALPHA][0:1]
         beta = state[BETA][0:1]
 
         def body(j, energy):
             base = pl.multiple_of((j + 1) * STEP, 8)
             flat = pl.ds(pl.multiple_of(j * ROWS, ROWS), ROWS)
-            value = bu[flat, :] - alpha * bw[flat, :]
-            if not final:
-                bu[flat, :] = value
-            value = value + beta * bq[flat, :]
+            value = bu[flat, :] + beta * bq[flat, :]
             here = cb[pl.ds(base, ROWS), :]
             stencil = (
                 sd[flat, :] * here
@@ -533,7 +529,7 @@
             to_scatter(j, base, value)
             return energy
 
-        return lax.fori_loop(0, BLOCKS, body, zero)
+        return lax.fori_loop(0, BLOCKS, body, zero, unroll=4)
 
 
     def widen_correction():
@@ -542,6 +538,8 @@
             pcf[case * FIELD : case * FIELD + FIELD, :] = wide[:, case * 128 : case * 128 + 128]
 
     def next_direction(final=False):
+        to_cases(0, state[ALPHA])
+        to_cases(1, state[BETA])
         widen_correction()
         kinds = 0 if final else 5
 

time: 84.4 us -> 83.9 us (level)
  no operation moved by 1% of the time
where the time goes in v5:
time: 83.9 us; the launch traced here: 83.7 us
  Pallas kernels  79.1 us (94%)
  other arithmetic  3.97 us (5%)
    pallas_call x1, Pallas kernels, shards(): pl.pallas_call(kernel, out_shape=[tall] * 4 + [jax.ShapeDtypeStruct((CASE...  79.1 us
    sub x1, other arithmetic, shards(): return (step + alpha * direction, rest - alpha * image)  3.97 us

profile of v5, /device:TPU:1, one launch (start us, length us, event | category | flops | bytes accessed | tf_op | source)
XLA Modules:
  0.0 83.7 jit_solution(7729361449217961012)
XLA Ops:
  0.6 79.1 %newton.1 = (f32[4,32,2048]{2,1,0:T(8,128)}, f32[4,32,2048]{2,1,0:T(8,128)}, f32[4,32,2048]{2,1,0:T(8,128)}, f32[4,32,2048]{2,1,0:T(8,128)}, f32[4,2048]{1,0:T(4,128)}) custom-call(f32[4,32,2048]{2,1,0:T(8,128)} %v_in.1, f32[4,32,2048]{2,1,0:T(8,128)} %photo_in.1, f32[32,2048]{1,0:T(8,128)} %shunt_in.1, f32[32,2048]{1,0:T(8,128)} %series_in.1, ...), custom_call_target="tpu_custom_call" | custom-call | tf_op jit(solution)/shard_map/newton/pallas_call | solution.py:712
  79.8 4.0 %multiply_subtract_fusion = (f32[4,32,2048]{2,1,0:T(8,128)}, f32[4,32,2048]{2,1,0:T(8,128)}) fusion(f32[4,32,2048]{2,1,0:T(8,128)} %get-tuple-element.10, f32[4,32,2048]{2,1,0:T(8,128)} %get-tuple-element.11, f32[4,2048]{1,0:T(4,128)} %get-tuple-element.8, f32[4,32,2048]{2,1,0:T(8,128)} %get-tuple-element.7, f32[4,32,2048]{2,1,0:T(8,128)} %get-tuple-element.9), kind=kLoop, calls=%fused_computation | loop fusion | flops 1048576 | bytes 6324224 | tf_op jit(solution)/shard_map/sub | solution.py:722

commit v6 on v5

--- a/solution.py
+++ b/solution.py
@@ -677,6 +677,29 @@
     arrived(fr.at[0 : NS * NC - 1], last_send.at[0])
 
 
+def last_update(step, direction, rest, image, alphas, step_out, rest_out, x, d, r, q, in_sem, out_sem):
+    loads = [
+        [pltpu.make_async_copy(src.at[case], dst.at[case], in_sem.at[i, case]) for i, (src, dst) in enumerate(pairs)]
+        for pairs in [((step, x), (direction, d), (rest, r), (image, q))]
+        for case in range(CASES)
+    ]
+    for copies in loads:
+        for copy in copies:
+            copy.start()
+    stores = []
+    for case in range(CASES):
+        for copy in loads[case]:
+            copy.wait()
+        alpha = alphas[case : case + 1, :]
+        x[case] = x[case] + alpha * d[case]
+        r[case] = r[case] - alpha * q[case]
+        for i, (src, dst) in enumerate(((x, step_out), (r, rest_out))):
+            stores.append(pltpu.make_async_copy(src.at[case], dst.at[case], out_sem.at[i, case]))
+            stores[-1].start()
+    for copy in stores:
+        copy.wait()
+
+
 def shards(voltage, photocurrent, shunt, series, pattern, diode_mask, aggregate, coarse_inverse):
     field = (CASES * FIELD, 128)
     flat = (BLOCKS * ROWS, 128)
@@ -718,8 +741,15 @@
         compiler_params=pltpu.CompilerParams(collective_id=0, has_side_effects=True, vmem_limit_bytes=54 * 2**20),
         name="newton",
     )(voltage, photocurrent, shunt, series, pattern.T, diode_mask.T, aggregate.T, coarse_inverse)
-    alpha = alpha[:, None, :]
-    return step + alpha * direction, rest - alpha * image
+    return pl.pallas_call(
+        last_update,
+        out_shape=[tall] * 2,
+        in_specs=[pl.BlockSpec(memory_space=pltpu.HBM)] * 4 + [pl.BlockSpec(memory_space=pltpu.VMEM)],
+        out_specs=[pl.BlockSpec(memory_space=pltpu.HBM)] * 2,
+        scratch_shapes=[vmem((CASES, ROWS, 2048)) for _ in range(4)] + [dma((4, CASES)), dma((2, CASES))],
+        compiler_params=pltpu.CompilerParams(vmem_limit_bytes=56 * 2**20),
+        name="last_update",
+    )(step, direction, rest, image, alpha)
 
 
 def solution(mesh):

time: 83.9 us -> 84 us (level)
  Pallas kernels: 79.1 us -> 83.1 us
  other arithmetic: 3.97 us -> 0 us
    pallas_call x0 -> x1, Pallas kernels: none -> 3.97 us  [shards(): pl.pallas_call(last_update, out_shape=[tall] * 2, in_specs=[pl.BlockSpec(...]
    sub x1 -> x0, other arithmetic: 3.97 us -> none  [shards(): return (step + alpha * direction, rest - alpha * image)]
where the time goes in v6:
time: 84 us; the launch traced here: 83.8 us
  Pallas kernels  83.1 us (99%)
    pallas_call x1, Pallas kernels, shards(): pl.pallas_call(kernel, out_shape=[tall] * 4 + [jax.ShapeDtypeStruct((CASE...  79.2 us
    pallas_call x1, Pallas kernels, shards(): pl.pallas_call(last_update, out_shape=[tall] * 2, in_specs=[pl.BlockSpec(...  3.97 us

profile of v6, /device:TPU:1, one launch (start us, length us, event | category | flops | bytes accessed | tf_op | source)
XLA Modules:
  0.0 83.8 jit_solution(4045137588153893976)
XLA Ops:
  0.6 79.2 %newton.1 = (f32[4,32,2048]{2,1,0:T(8,128)}, f32[4,32,2048]{2,1,0:T(8,128)}, f32[4,32,2048]{2,1,0:T(8,128)}, f32[4,32,2048]{2,1,0:T(8,128)}, f32[4,2048]{1,0:T(4,128)}) custom-call(f32[4,32,2048]{2,1,0:T(8,128)} %v_in.1, f32[4,32,2048]{2,1,0:T(8,128)} %photo_in.1, f32[32,2048]{1,0:T(8,128)} %shunt_in.1, f32[32,2048]{1,0:T(8,128)} %series_in.1, ...), custom_call_target="tpu_custom_call" | custom-call | tf_op jit(solution)/shard_map/newton/pallas_call | solution.py:735
  79.8 4.0 %last_update.1 = (f32[4,32,2048]{2,1,0:T(8,128)}, f32[4,32,2048]{2,1,0:T(8,128)}) custom-call(f32[4,32,2048]{2,1,0:T(8,128)} %get-tuple-element.7.step, f32[4,32,2048]{2,1,0:T(8,128)} %get-tuple-element.8.direction, f32[4,32,2048]{2,1,0:T(8,128)} %get-tuple-element.9.rest, f32[4,32,2048]{2,1,0:T(8,128)} %get-tuple-element.10.image, ...), custom_call_target="tpu_custom_call" | custom-call | tf_op jit(solution)/shard_map/last_update/pallas_call | solution.py:744
